TPU v7x, 32 devices: a whole 2x2x4 slice. The times are simulated.
32 devices in a mesh: groups: 2 (over y), blocks: 8 (over z, x), span: 2 (over core).
Axes of the slice: x: 2, y: 2, z: 4, core: 2. Of those that a mesh axis runs over, the one named last changes fastest.
Arguments:
- state: float32 [9, 6, 16, 2, 8, 512], P(None, None, ('groups', 'blocks'), None, None, 'span'), parts along dimension 2, may hold values from -4 to 4
- source: float32 [9, 6, 16, 2, 8, 512], P(None, None, ('groups', 'blocks'), None, None, 'span'), parts along dimension 2, may hold values from -6 to 6
- block_matrix: float32 [6, 6, 16, 2, 8, 512], P(None, None, ('groups', 'blocks'), None, None, 'span'), parts along dimension 2, may hold values from -1 to 16, as said below
- phase_index: int32 [8], P('groups'), parts along dimension 0, may hold values from 1 to 63
- face_pair: int32 [2048], replicated, may hold values from 0 to 2047, each once
Outputs:
- new_state: float32 [9, 6, 16, 2, 8, 512], P(None, None, ('groups', 'blocks'), None, None, 'span'), parts along dimension 2
- residual: float32 [9, 6, 16, 2, 8, 512], P(None, None, ('groups', 'blocks'), None, None, 'span'), parts along dimension 2
There are 2 independent parts, one for each index of `groups`. A program takes and returns all parts, laid end to end along the dimension named above; an argument that names none is the same for every part. Nothing has to cross between parts.
Inputs may be any that keep to these rules, and one draw needn't show every extreme that they name: `block_matrix`: entries whose two variable indices are equal lie between 10 and 16; all others between -1 and 1.
All inputs are finite; a program needn't handle non-finite values.
Results may differ from a plain program's by a relative error of at most 0.0001.
Values sent between devices are 32-bit elements; how exact they have to be, the bound alone decides.
No kernel may reach another device: no remote copies, remote signals or barrier semaphores. Data moves between devices by JAX's collectives and lax.ppermute only.
A program may use at most 64 MiB of HBM per device.

v0:
```python
import math

import jax
import jax.numpy as jnp
from jax import lax
from jax.sharding import PartitionSpec as P

NPASS = 64
AXB = 2
NSWEEP = 3


def from_behind(block, axis, distance):
    devices = range(lax.axis_size(axis))
    route = [((i - distance) % len(devices), i) for i in devices]
    return lax.ppermute(block, axis, route)


def partner_2(block, axis, distance):
    count = lax.axis_size(axis)
    route = []
    for low in range(count):
        high = low | 1 << distance
        if high != low and high < count:
            route += [(low, high), (high, low)]
    return lax.ppermute(block, axis, route)


def passed_along(block, axis, distance):
    devices = range(lax.axis_size(axis))
    route = [(i - distance, i) for i in devices if i - distance in devices]
    return lax.ppermute(block, axis, route)


def instance_tables(phase_index, instances):
    harmonics = (instances - 1) // 2
    angles = 2.0 * math.pi * jnp.arange(instances, dtype=jnp.float32) / instances
    spacing = angles[:, None] - angles[None, :]
    orders = jnp.arange(1, harmonics + 1, dtype=jnp.float32)
    phases = 2.0 * math.pi * phase_index.astype(jnp.float32) / NPASS
    argument = orders[:, None, None] * spacing[None]
    shift_plus = (
        1.0 + 2.0 * jnp.sum(jnp.cos(argument + phases[:, None, None]), axis=0)
    ) / instances
    shift_minus = (
        1.0 + 2.0 * jnp.sum(jnp.cos(argument - phases[:, None, None]), axis=0)
    ) / instances
    spectral = -(2.0 / instances) * jnp.sum(orders[:, None, None] * jnp.sin(argument), axis=0)
    return (shift_plus, shift_minus, spectral)


def mix_instances(matrix, state_now):
    return lax.dot_general(
        matrix,
        state_now,
        (((1,), (0,)), ((), ())),
        precision=lax.Precision.HIGHEST,
        preferred_element_type=jnp.float32,
    )


def apply_block(matrix, state_now):
    accum_term = matrix[None, :, 0] * state_now[:, None, 0]
    for column in range(1, state_now.shape[1]):
        accum_term = accum_term + matrix[None, :, column] * state_now[:, None, column]
    return accum_term


def split_block(matrix):
    variables = matrix.shape[0]
    picker = jnp.arange(variables)[:, None] == jnp.arange(variables)[None, :]
    picker = picker.reshape((variables, variables) + (1,) * (matrix.ndim - 2))
    offblock = jnp.where(picker, jnp.zeros_like(matrix), matrix)
    diagonal = jnp.stack([matrix[variable, variable] for variable in range(variables)])
    return (diagonal, offblock)


def point_solve(residual, diagonal, offblock, spectral):
    result = residual / diagonal[None]
    for sweep_index in range(NSWEEP):
        result = (
            residual - apply_block(offblock, result) - mix_instances(spectral, result)
        ) / diagonal[None]
    return result


def neighbour_sum(state_now, ghosts):
    lower_circ, upper_circ, lower_axial, upper_axial, lower_span, upper_span = ghosts
    near_sum = jnp.concatenate([lower_circ[:, :, None], state_now[:, :, :-1]], axis=2)
    near_sum = near_sum + jnp.concatenate([state_now[:, :, 1:], upper_circ[:, :, None]], axis=2)
    near_sum = near_sum + jnp.concatenate(
        [lower_axial[:, :, :, None], state_now[:, :, :, :-1]], axis=3
    )
    near_sum = near_sum + jnp.concatenate(
        [state_now[:, :, :, 1:], upper_axial[:, :, :, None]], axis=3
    )
    near_sum = near_sum + jnp.concatenate([lower_span[..., None], state_now[..., :-1]], axis=4)
    near_sum = near_sum + jnp.concatenate([state_now[..., 1:], upper_span[..., None]], axis=4)
    return near_sum


def pair_table(pairing, axial_cells, span_cells):
    wanted = pairing.reshape(axial_cells, span_cells, 1, 1)
    source_cell = lax.broadcasted_iota(
        jnp.int32, (1, 1, axial_cells, span_cells), 2
    ) * span_cells + lax.broadcasted_iota(jnp.int32, (1, 1, axial_cells, span_cells), 3)
    return (wanted == source_cell).astype(jnp.float32)


def pair_face(face_layer, table, rotation):
    picked = jnp.einsum(
        "iltp,outp->ilou",
        face_layer,
        table,
        precision=lax.Precision.HIGHEST,
        preferred_element_type=jnp.float32,
    )
    return mix_instances(rotation, picked)


def shards(state, source, block_matrix, phase_index, face_pair):
    state_now = state[:, :, 0]
    forcing = source[:, :, 0]
    matrix = block_matrix[:, :, 0]
    shift_plus, shift_minus, spectral = instance_tables(phase_index, state_now.shape[0])
    axial_cells = state_now.shape[3]
    span_cells = state_now.shape[4]
    inverse = (
        jnp.zeros_like(face_pair).at[face_pair].set(jnp.arange(face_pair.shape[0], dtype=jnp.int32))
    )
    forward_table = pair_table(face_pair, axial_cells, span_cells)
    inverse_table = pair_table(inverse, axial_cells, span_cells)
    position = lax.axis_index("blocks")
    circ_count = lax.axis_size("blocks") // AXB
    circ_place = position // AXB
    axial_place = position % AXB
    at_first = circ_place == 0
    at_last = circ_place == circ_count - 1
    top_layer = state_now[:, :, -1]
    bottom_layer = state_now[:, :, 0]
    lower_circ = from_behind(top_layer, "blocks", AXB)
    upper_circ = from_behind(bottom_layer, "blocks", -AXB)
    lower_circ = jnp.where(at_first, pair_face(lower_circ, forward_table, shift_minus), lower_circ)
    upper_circ = jnp.where(at_last, pair_face(upper_circ, inverse_table, shift_plus), upper_circ)
    facing = jnp.where(axial_place == 0, state_now[:, :, :, -1], state_now[:, :, :, 0])
    partner = partner_2(facing, "blocks", 0)
    zero_axial = jnp.zeros_like(partner)
    lower_axial = jnp.where(axial_place == 1, partner, zero_axial)
    upper_axial = jnp.where(axial_place == 0, partner, zero_axial)
    lower_span = passed_along(state_now[..., -1], "span", 1)
    upper_span = passed_along(state_now[..., 0], "span", -1)
    ghosts = (lower_circ, upper_circ, lower_axial, upper_axial, lower_span, upper_span)
    local_term = apply_block(matrix, state_now)
    time_term = mix_instances(spectral, state_now)
    diagonal, offblock = split_block(matrix)
    near_sum = neighbour_sum(state_now, ghosts)
    residual = forcing - (local_term - near_sum + time_term)
    update = point_solve(residual, diagonal, offblock, spectral)
    new_state = state_now + update
    return (new_state[:, :, None], residual[:, :, None])


def solution(mesh):
    placed = (
        P(None, None, ("groups", "blocks"), None, None, "span"),
        P(None, None, ("groups", "blocks"), None, None, "span"),
        P(None, None, ("groups", "blocks"), None, None, "span"),
        P("groups"),
        P(),
    )
    return jax.shard_map(
        shards,
        mesh=mesh,
        in_specs=placed,
        out_specs=(
            P(None, None, ("groups", "blocks"), None, None, "span"),
            P(None, None, ("groups", "blocks"), None, None, "span"),
        ),
        check_vma=False,
    )
```

profile of v0, /device:TPU:1, one launch (start us, length us, event | category | flops | bytes accessed | tf_op | source)
XLA Modules:
  0.0 84.4 jit_solution(12621772648586783437)
XLA Ops:
  0.6 1.7 %fusion.86 = (f32[9,6,2,1,256]{4,3,2,1,0:T(1,128)S(1)}, f32[9,6,2,1,256]{4,3,2,1,0:T(1,128)S(1)}) fusion(f32[9,6,2,8,256]{4,3,2,1,0:T(8,128)} %bitcast.199), kind=kLoop, calls=%fused_computation.150 | loop fusion | bytes 442368 | tf_op jit(solution)/shard_map/slice | solution.py:145
  2.3 0.7 fusion.31
  3.1 2.0 %collective-permute-start.2 = (f32[9,6,2,256]{3,0,1,2:T(8,128)}, f32[9,6,2,256]{3,0,1,2:T(8,128)}, u32[]{:S(2)}, u32[]{:S(2)}) collective-permute-start(f32[9,6,2,256]{3,0,1,2:T(8,128)} %fusion.31), channel_id=1, source_target_pairs={{0,2},{2,0},{4,6},{6,4},{8,10},{10,8},{12,14},{14,12},{1,3},{3,1},... | collective-permute-start | bytes 331784 | tf_op jit(solution)/shard_map/ppermute | solution.py:26
  5.1 1.7 %copy.286 = f32[9,6,1,2,8,256]{5,0,4,1,3,2:T(8,128)S(1)} copy(f32[9,6,1,2,8,256]{5,4,3,2,1,0:T(8,128)} %param.5) | data formatting | bytes 1769472 | tf_op args[0]
  6.8 1.4 %fusion.85 = (f32[9,6,1,8,256]{4,0,3,1,2:T(8,128)}, f32[9,6,8,256]{3,0,2,1:T(8,128)S(1)}, f32[9,6,8,256]{3,0,2,1:T(8,128)S(1)}, f32[9,6,1,8,256]{4,0,3,1,2:T(8,128)}) fusion(f32[9,6,2,8,256]{4,0,3,1,2:T(8,128)S(1)} %bitcast.186), kind=kLoop, calls=%fused_computation.149 | loop fusion | bytes 2654208 | tf_op jit(solution)/shard_map/slice | solution.py:139
  8.2 1.0 %copy.155 = f32[9,6,8,256]{3,2,1,0:T(8,128)} copy(f32[9,6,8,256]{3,0,2,1:T(8,128)S(1)} %get-tuple-element.47) | data formatting | bytes 884736 | tf_op jit(solution)/shard_map/squeeze | solution.py:140
  9.2 3.3 %collective-permute-start.1 = (f32[9,6,8,256]{3,2,1,0:T(8,128)}, f32[9,6,8,256]{3,2,1,0:T(8,128)}, u32[]{:S(2)}, u32[]{:S(2)}) collective-permute-start(f32[9,6,8,256]{3,2,1,0:T(8,128)} %copy.155), channel_id=1, source_target_pairs={{4,0},{6,2},{8,4},{10,6},{12,8},{14,10},{0,12},{2,14},{5,1},{7,3},... | collective-permute-start | bytes 1327112 | tf_op jit(solution)/shard_map/ppermute | solution.py:16
  12.6 1.0 %copy.151 = f32[9,6,8,256]{3,2,1,0:T(8,128)} copy(f32[9,6,8,256]{3,0,2,1:T(8,128)S(1)} %get-tuple-element.46) | data formatting | bytes 884736 | tf_op jit(solution)/shard_map/squeeze | solution.py:139
  14.5 1.3 %collective-permute-start.3 = (f32[9,6,2,8]{0,3,2,1:T(8,128)S(1)}, f32[9,6,2,8]{0,3,2,1:T(8,128)}, u32[]{:S(2)}, u32[]{:S(2)}) collective-permute-start(f32[9,6,2,8]{0,3,2,1:T(8,128)S(1)} %bitcast.201), channel_id=1, source_target_pairs={{0,1},{2,3},{4,5},{6,7},{8,9},{10,11},{12,13},{14,15},{16,17},{18,... | collective-permute-start | bytes 10376 | tf_op jit(solution)/shard_map/ppermute | solution.py:32
  15.8 1.3 %copy.164 = f32[9,6,2,8,1]{0,3,4,2,1:T(8,128)} copy(f32[9,6,2,8,1]{4,0,3,1,2:T(8,128)S(1)} %get-tuple-element.41) | data formatting | bytes 6912 | tf_op jit(solution)/shard_map/slice | solution.py:151
  17.1 4.4 %collective-permute-start.4 = (f32[9,6,2,8]{0,3,2,1:T(8,128)}, f32[9,6,2,8]{0,3,2,1:T(8,128)}, u32[]{:S(2)}, u32[]{:S(2)}) collective-permute-start(f32[9,6,2,8]{0,3,2,1:T(8,128)} %bitcast.43), channel_id=1, source_target_pairs={{1,0},{3,2},{5,4},{7,6},{9,8},{11,10},{13,12},{15,14},{17,16},{19,... | collective-permute-start | bytes 10376 | tf_op jit(solution)/shard_map/ppermute | solution.py:32
  21.5 0.7 fusion.43
  22.2 2.0 %slice_bitcast_fusion.35 = (f32[6,2,8,256]{3,2,1,0:T(8,128)}, f32[6,2,8,256]{3,2,1,0:T(8,128)}, f32[6,2,8,256]{3,2,1,0:T(8,128)}, f32[6,2,8,256]{3,2,1,0:T(8,128...) fusion(f32[6,6,2,8,256]{4,3,2,1,0:T(8,128)} %bitcast.192), kind=kLoop, calls=%fused_computation.76 | loop fusion | bytes 1179648 | tf_op jit(solution)/shard_map/mul | solution.py:63
  24.2 1.1 %slice_bitcast_fusion.23 = (f32[9,2,8,256]{3,0,2,1:T(8,128)S(1)}, f32[9,2,8,256]{3,0,2,1:T(8,128)}, f32[9,2,8,256]{3,0,2,1:T(8,128)}, f32[9,2,8,256]{3,0,2,1:T(8...) fusion(f32[9,6,2,8,256]{4,0,3,1,2:T(8,128)S(1)} %bitcast.188), kind=kLoop, calls=%fused_computation.60 | loop fusion | bytes 1769472 | tf_op jit(solution)/shard_map/mul | solution.py:63
  25.3 1.8 %fusion.82 = (f32[9,6,2,8,255]{4,0,3,1,2:T(8,128)S(1)}, f32[9,6,2,8,255]{4,0,3,1,2:T(8,128)}) fusion(f32[9,6,2,8,256]{4,0,3,1,2:T(8,128)S(1)} %bitcast.189), kind=kLoop, calls=%fused_computation.146 | loop fusion | bytes 3525120 | tf_op jit(solution)/shard_map/slice | solution.py:98
  27.1 1.9 %fusion.84 = (f32[9,6,2,7,256]{4,0,3,1,2:T(8,128)}, f32[9,6,2,7,256]{4,0,3,1,2:T(8,128)}) fusion(f32[9,6,2,8,256]{4,0,3,1,2:T(8,128)S(1)} %bitcast.190), kind=kLoop, calls=%fused_computation.148 | loop fusion | bytes 3096576 | tf_op jit(solution)/shard_map/slice | solution.py:95
  29.3 0.8 slice_bitcast_fusion.29
  30.1 1.0 %fusion.35 = (f32[9,9]{1,0:T(8,128)}, f32[9,9]{1,0:T(8,128)}, f32[9,9]{1,0:T(8,128)S(1)}) fusion(f32[4]{0:T(128)S(1)} %get-tuple-element.67, f32[9,9]{1,0:T(8,128)S(1)} %broadcast_subtract_fusion, f32[4]{0:T(128)S(1)} %get-tuple-element.68), kind=kLoop, calls=%fused_computation.84 | loop fusion | flops 2025 | bytes 1328 | tf_op jit(solution)/shard_map/reduce_sum | solution.py:43
  31.2 8.2 %scatter_custom_fusion = s32[2048]{0:T(1024)S(1)} fusion(s32[2048]{0:T(1024)S(1)} %compare_select_fusion, s32[2048]{0:T(1024)S(1)} %iota.65, s32[]{:T(128)} %constant.51.clone.1), kind=kCustom, calls=%fused_computation.121 | custom fusion | bytes 8196 | tf_op jit(solution)/shard_map/scatter | solution.py:129
  39.5 1.5 %copy.163 = f32[9,6,2,8,1]{4,0,3,1,2:T(8,128)S(1)} copy(f32[9,6,2,8,1]{0,3,4,2,1:T(8,128)} %bitcast.42) | data formatting | bytes 6912 | tf_op jit(solution)/shard_map/broadcast_in_dim | solution.py:97
  41.0 1.5 %copy.165 = f32[9,6,2,8,1]{4,0,3,1,2:T(8,128)S(1)} copy(f32[9,6,2,8,1]{0,3,4,2,1:T(8,128)} %bitcast.44) | data formatting | bytes 6912 | tf_op jit(solution)/shard_map/broadcast_in_dim | solution.py:98
  42.5 1.0 %select_bitcast_fusion = (f32[9,6,2,1,256]{4,0,3,1,2:T(8,128)S(1)}, f32[9,6,2,1,256]{4,0,3,1,2:T(8,128)S(1)}) fusion(f32[9,6,2,256]{3,0,1,2:T(8,128)} %collective-permute-done.2, pred[]{:T(512)S(6)} %eq.72, pred[]{:T(512)S(6)} %eq.71), kind=kLoop, calls=%fused_computation.63 | loop fusion | flops 55296 | bytes 331778 | tf_op jit(solution)/shard_map/broadcast_in_dim | solution.py:95
  43.4 9.2 %fusion.26 = f32[9,6,8,256]{3,0,1,2:T(8,128)S(1)} fusion(s32[8,256]{1,0:T(8,128)S(1)} %eq.68, s32[8,256]{1,0:T(8,128)S(1)} %iota_add_fusion, f32[9,6,8,256]{3,2,1,0:T(8,128)} %collective-permute-done.1), kind=kOutput, calls=%fused_computation.30 | convolution fusion | flops 2722103296 | bytes 901120 | tf_op jit(solution)/shard_map/iltp,outp->ilou/dot_general | solution.py:111
  52.8 9.6 %fusion.23 = f32[9,6,8,256]{3,0,1,2:T(8,128)S(1)} fusion(s32[8,256]{1,0:T(8,128)S(1)} %iota_add_fusion, s32[8,256]{1,0:T(8,128)S(1)} %eq.63, f32[9,6,8,256]{3,2,1,0:T(8,128)} %collective-permute-done), kind=kOutput, calls=%fused_computation.29 | convolution fusion | flops 2722103296 | bytes 901120 | tf_op jit(solution)/shard_map/iltp,outp->ilou/dot_general | solution.py:111
  62.5 2.1 %fusion.21 = f32[9,6,1,8,256]{4,0,3,1,2:T(8,128)S(1)} fusion(f32[9,6,8,256]{3,2,1,0:T(8,128)} %collective-permute-done.1, f32[9,6,8,256]{3,0,1,2:T(8,128)S(1)} %fusion.26, pred[]{:T(512)S(6)} %eq.67, f32[9,9]{1,0:T(8,128)S(1)} %copy-done.26), kind=kOutput, calls=%fused_computation.26 | convolution fusion | flops 12054771 | bytes 1327429 | tf_op jit(solution)/shard_map/dot_general | solution.py:53
  64.6 2.1 %fusion.22 = f32[9,6,1,8,256]{4,0,3,1,2:T(8,128)S(1)} fusion(f32[9,6,8,256]{3,2,1,0:T(8,128)} %collective-permute-done, f32[9,6,8,256]{3,0,1,2:T(8,128)S(1)} %fusion.23, pred[]{:T(512)S(6)} %eq.62, f32[9,9]{1,0:T(8,128)S(1)} %copy-done.25), kind=kOutput, calls=%fused_computation.28 | convolution fusion | flops 12054771 | bytes 1327429 | tf_op jit(solution)/shard_map/dot_general | solution.py:53
  67.0 4.1 %broadcast_divide_fusion = (f32[9,6,2,8,256]{4,0,3,1,2:T(8,128)S(1)}, f32[9,6,2,8,256]{4,0,3,1,2:T(8,128)S(1)}) fusion(f32[9,6,2,8,256]{4,3,2,1,0:T(8,128)S(1)} %bitcast.200, f32[9,9]{1,0:T(8,128)S(1)} %get-tuple-element.14, f32[9,6,2,8,1]{4,0,3,1,2:T(8,128)S(1)} %copy.165, f32[9,6,2,8,255]{4,0,3,1,2:T(8,128)S(1)} %get-tuple-element.39, ...), kind=kOutput, calls=%fused_computation.35 | convolution fusion | flops 29638736 | bytes 10420548 | tf_op jit(solution)/shard_map/dot_general | solution.py:53
  72.2 2.8 %subtract_divide_fusion.1 = f32[9,6,2,8,256]{4,0,3,1,2:T(8,128)S(1)} fusion(f32[9,6,2,8,256]{4,0,3,1,2:T(8,128)S(1)} %get-tuple-element.66, f32[9,2,8,256]{3,0,2,1:T(8,128)S(1)} %get-tuple-element.28, f32[9,2,8,256]{3,0,2,1:T(8,128)S(1)} %get-tuple-element.29, f32[9,2,8,256]{3,0,2,1:T(8,128)S(1)} %get-tuple-element.30, ...), kind=kOutput, calls=%fused_computation.24 | convolution fusion | flops 27205712 | bytes 3342660 | tf_op jit(solution)/shard_map/dot_general | solution.py:53
  75.1 2.7 %subtract_divide_fusion = f32[9,6,2,8,256]{4,0,3,1,2:T(8,128)S(1)} fusion(f32[9,6,2,8,256]{4,0,3,1,2:T(8,128)S(1)} %get-tuple-element.66, f32[9,6,2,8,256]{4,0,3,1,2:T(8,128)S(1)} %subtract_divide_fusion.1, f32[9,2,8,256]{3,0,2,1:T(8,128)S(1)} %get-tuple-element.22, f32[9,2,8,256]{3,0,2,1:T(8,128)S(1)} %get-tuple-element.23, ...), kind=kOutput, calls=%fused_computation.23 | convolution fusion | flops 26984528 | bytes 4227396 | tf_op jit(solution)/shard_map/dot_general | solution.py:53
  78.0 3.5 %add_bitcast_fusion = f32[9,6,1,2,8,256]{5,0,4,1,3,2:T(8,128)S(1)} fusion(f32[9,6,2,8,256]{4,0,3,1,2:T(8,128)S(1)} %get-tuple-element.66, f32[9,6,2,8,256]{4,0,3,1,2:T(8,128)S(1)} %subtract_divide_fusion, f32[9,2,8,256]{3,0,2,1:T(8,128)S(1)} %get-tuple-element.16, f32[9,2,8,256]{3,0,2,1:T(8,128)S(1)} %get-tuple-element.17, ...), kind=kOutput, calls=%fused_computation.22 | convolution fusion | flops 27205712 | bytes 5112132 | tf_op jit(solution)/shard_map/dot_general | solution.py:53
  81.5 1.4 %copy.181 = f32[9,6,1,2,8,256]{5,4,3,2,1,0:T(8,128)} copy(f32[9,6,1,2,8,256]{5,0,4,1,3,2:T(8,128)S(1)} %add_bitcast_fusion) | data formatting | bytes 1769472
  83.0 1.4 %copy.182 = f32[9,6,1,2,8,256]{5,4,3,2,1,0:T(8,128)} copy(f32[9,6,1,2,8,256]{5,0,4,1,3,2:T(8,128)S(1)} %bitcast.198) | data formatting | bytes 1769472
  (89 shorter events, 2.7 us)
Async XLA Ops:
  3.1 39.4 %collective-permute-start.2 = (f32[9,6,2,256]{3,0,1,2:T(8,128)}, f32[9,6,2,256]{3,0,1,2:T(8,128)}, u32[]{:S(2)}, u32[]{:S(2)}) collective-permute-start(f32[9,6,2,256]{3,0,1,2:T(8,128)} %fusion.31), channel_id=1, source_target_pairs={{0,2},{2,0},{4,6},{6,4},{8,10},{10,8},{12,14},{14,12},{1,3},{3,1},... | collective-permute-start | bytes 331784 | tf_op jit(solution)/shard_map/ppermute | solution.py:26
  9.2 34.2 %collective-permute-start.1 = (f32[9,6,8,256]{3,2,1,0:T(8,128)}, f32[9,6,8,256]{3,2,1,0:T(8,128)}, u32[]{:S(2)}, u32[]{:S(2)}) collective-permute-start(f32[9,6,8,256]{3,2,1,0:T(8,128)} %copy.155), channel_id=1, source_target_pairs={{4,0},{6,2},{8,4},{10,6},{12,8},{14,10},{0,12},{2,14},{5,1},{7,3},... | collective-permute-start | bytes 1327112 | tf_op jit(solution)/shard_map/ppermute | solution.py:16
  13.6 39.1 %collective-permute-start = (f32[9,6,8,256]{3,2,1,0:T(8,128)}, f32[9,6,8,256]{3,2,1,0:T(8,128)}, u32[]{:S(2)}, u32[]{:S(2)}) collective-permute-start(f32[9,6,8,256]{3,2,1,0:T(8,128)} %copy.151), channel_id=1, source_target_pairs={{12,0},{14,2},{0,4},{2,6},{4,8},{6,10},{8,12},{10,14},{13,1},{15,3... | collective-permute-start | bytes 1327112 | tf_op jit(solution)/shard_map/ppermute | solution.py:16
  14.5 24.9 %collective-permute-start.3 = (f32[9,6,2,8]{0,3,2,1:T(8,128)S(1)}, f32[9,6,2,8]{0,3,2,1:T(8,128)}, u32[]{:S(2)}, u32[]{:S(2)}) collective-permute-start(f32[9,6,2,8]{0,3,2,1:T(8,128)S(1)} %bitcast.201), channel_id=1, source_target_pairs={{0,1},{2,3},{4,5},{6,7},{8,9},{10,11},{12,13},{14,15},{16,17},{18,... | collective-permute-start | bytes 10376 | tf_op jit(solution)/shard_map/ppermute | solution.py:32
  17.1 23.8 %collective-permute-start.4 = (f32[9,6,2,8]{0,3,2,1:T(8,128)}, f32[9,6,2,8]{0,3,2,1:T(8,128)}, u32[]{:S(2)}, u32[]{:S(2)}) collective-permute-start(f32[9,6,2,8]{0,3,2,1:T(8,128)} %bitcast.43), channel_id=1, source_target_pairs={{1,0},{3,2},{5,4},{7,6},{9,8},{11,10},{13,12},{15,14},{17,16},{19,... | collective-permute-start | bytes 10376 | tf_op jit(solution)/shard_map/ppermute | solution.py:32
  27.1 2.0 %copy-start.23 = (s32[2048]{0:T(1024)S(1)}, s32[2048]{0:T(1024)}, u32[]{:S(2)}) copy-start(s32[2048]{0:T(1024)} %param.9) | copy-start | bytes 24580
  27.1 2.1 %copy-start = (f32[6,6,1,2,8,256]{5,4,3,2,1,0:T(8,128)S(1)}, f32[6,6,1,2,8,256]{5,4,3,2,1,0:T(8,128)}, u32[]{:S(2)}) copy-start(f32[6,6,1,2,8,256]{5,4,3,2,1,0:T(8,128)} %param.7) | copy-start | bytes 1769476
  29.0 1.2 %copy-start.30 = (s32[4]{0:T(128)S(1)}, s32[4]{0:T(128)}, u32[]{:S(2)}) copy-start(s32[4]{0:T(128)} %param.8) | copy-start | bytes 52
  29.0 2.2 %copy-start.24 = (s32[2048]{0:T(1024)S(1)}, s32[2048]{0:T(1024)}, u32[]{:S(2)}) copy-start(s32[2048]{0:T(1024)} %param.9) | copy-start | bytes 24580
  52.7 9.8 %copy-start.26 = (f32[9,9]{1,0:T(8,128)S(1)}, f32[9,9]{1,0:T(8,128)}, u32[]{:S(2)}) copy-start(f32[9,9]{1,0:T(8,128)} %get-tuple-element.12) | copy-start | bytes 976
  52.7 14.1 %copy-start.4 = (f32[9,6,2,7,256]{4,0,3,1,2:T(8,128)S(1)}, f32[9,6,2,7,256]{4,0,3,1,2:T(8,128)}, u32[]{:S(2)}) copy-start(f32[9,6,2,7,256]{4,0,3,1,2:T(8,128)} %get-tuple-element.44) | copy-start | bytes 2322436
  52.7 14.1 %copy-start.6 = (f32[9,6,1,8,256]{4,0,3,1,2:T(8,128)S(1)}, f32[9,6,1,8,256]{4,0,3,1,2:T(8,128)}, u32[]{:S(2)}) copy-start(f32[9,6,1,8,256]{4,0,3,1,2:T(8,128)} %get-tuple-element.48) | copy-start | bytes 1327108
  52.7 14.1 %copy-start.7 = (f32[9,2,8,256]{3,0,2,1:T(8,128)S(1)}, f32[9,2,8,256]{3,0,2,1:T(8,128)}, u32[]{:S(2)}) copy-start(f32[9,2,8,256]{3,0,2,1:T(8,128)} %get-tuple-element.34) | copy-start | bytes 442372
  52.7 14.1 %copy-start.8 = (f32[9,2,8,256]{3,0,2,1:T(8,128)S(1)}, f32[9,2,8,256]{3,0,2,1:T(8,128)}, u32[]{:S(2)}) copy-start(f32[9,2,8,256]{3,0,2,1:T(8,128)} %get-tuple-element.35) | copy-start | bytes 442372
  52.7 14.1 %copy-start.9 = (f32[9,2,8,256]{3,0,2,1:T(8,128)S(1)}, f32[9,2,8,256]{3,0,2,1:T(8,128)}, u32[]{:S(2)}) copy-start(f32[9,2,8,256]{3,0,2,1:T(8,128)} %get-tuple-element.36) | copy-start | bytes 442372
  52.7 14.1 %copy-start.10 = (f32[9,2,8,256]{3,0,2,1:T(8,128)S(1)}, f32[9,2,8,256]{3,0,2,1:T(8,128)}, u32[]{:S(2)}) copy-start(f32[9,2,8,256]{3,0,2,1:T(8,128)} %get-tuple-element.37) | copy-start | bytes 442372
  52.7 14.1 %copy-start.11 = (f32[9,2,8,256]{3,0,2,1:T(8,128)S(1)}, f32[9,2,8,256]{3,0,2,1:T(8,128)}, u32[]{:S(2)}) copy-start(f32[9,2,8,256]{3,0,2,1:T(8,128)} %get-tuple-element.38) | copy-start | bytes 442372
  52.8 14.1 %copy-start.18 = (f32[6,2,8,256]{3,2,1,0:T(8,128)S(1)}, f32[6,2,8,256]{3,2,1,0:T(8,128)}, u32[]{:S(2)}) copy-start(f32[6,2,8,256]{3,2,1,0:T(8,128)} %get-tuple-element.58) | copy-start | bytes 294916
  52.8 14.1 %copy-start.19 = (f32[6,2,8,256]{3,2,1,0:T(8,128)S(1)}, f32[6,2,8,256]{3,2,1,0:T(8,128)}, u32[]{:S(2)}) copy-start(f32[6,2,8,256]{3,2,1,0:T(8,128)} %get-tuple-element.59) | copy-start | bytes 294916
  52.8 14.1 %copy-start.20 = (f32[6,2,8,256]{3,2,1,0:T(8,128)S(1)}, f32[6,2,8,256]{3,2,1,0:T(8,128)}, u32[]{:S(2)}) copy-start(f32[6,2,8,256]{3,2,1,0:T(8,128)} %get-tuple-element.60) | copy-start | bytes 294916
  52.8 14.1 %copy-start.21 = (f32[6,2,8,256]{3,2,1,0:T(8,128)S(1)}, f32[6,2,8,256]{3,2,1,0:T(8,128)}, u32[]{:S(2)}) copy-start(f32[6,2,8,256]{3,2,1,0:T(8,128)} %get-tuple-element.61) | copy-start | bytes 294916
  52.8 14.1 %copy-start.22 = (f32[6,2,8,256]{3,2,1,0:T(8,128)S(1)}, f32[6,2,8,256]{3,2,1,0:T(8,128)}, u32[]{:S(2)}) copy-start(f32[6,2,8,256]{3,2,1,0:T(8,128)} %get-tuple-element.62) | copy-start | bytes 294916
  52.8 14.1 %copy-start.28 = (f32[6,2,8,256]{3,2,1,0:T(8,128)S(1)}, f32[6,2,8,256]{3,2,1,0:T(8,128)}, u32[]{:S(2)}) copy-start(f32[6,2,8,256]{3,2,1,0:T(8,128)} %copy-done.27) | copy-start | bytes 294916
  52.8 14.1 %copy-start.29 = (f32[9,6,1,2,8,256]{5,4,3,2,1,0:T(8,128)S(1)}, f32[9,6,1,2,8,256]{5,4,3,2,1,0:T(8,128)}, u32[]{:S(2)}) copy-start(f32[9,6,1,2,8,256]{5,4,3,2,1,0:T(8,128)} %param.6) | copy-start | bytes 2654212
  62.4 2.2 %copy-start.25 = (f32[9,9]{1,0:T(8,128)S(1)}, f32[9,9]{1,0:T(8,128)}, u32[]{:S(2)}) copy-start(f32[9,9]{1,0:T(8,128)} %get-tuple-element.13) | copy-start | bytes 976
  62.4 4.5 %copy-start.2 = (f32[9,6,1,2,8,256]{5,4,3,2,1,0:T(8,128)S(1)}, f32[9,6,1,2,8,256]{5,4,3,2,1,0:T(8,128)}, u32[]{:S(2)}) copy-start(f32[9,6,1,2,8,256]{5,4,3,2,1,0:T(8,128)} %param.5) | copy-start | bytes 2654212
  62.4 4.5 %copy-start.3 = (f32[9,6,2,7,256]{4,0,3,1,2:T(8,128)S(1)}, f32[9,6,2,7,256]{4,0,3,1,2:T(8,128)}, u32[]{:S(2)}) copy-start(f32[9,6,2,7,256]{4,0,3,1,2:T(8,128)} %get-tuple-element.43) | copy-start | bytes 2322436
  62.5 4.5 %copy-start.17 = (f32[6,2,8,256]{3,2,1,0:T(8,128)S(1)}, f32[6,2,8,256]{3,2,1,0:T(8,128)}, u32[]{:S(2)}) copy-start(f32[6,2,8,256]{3,2,1,0:T(8,128)} %get-tuple-element.57) | copy-start | bytes 294916
  64.6 2.3 %copy-start.1 = (f32[9,6,2,8,255]{4,0,3,1,2:T(8,128)S(1)}, f32[9,6,2,8,255]{4,0,3,1,2:T(8,128)}, u32[]{:S(2)}) copy-start(f32[9,6,2,8,255]{4,0,3,1,2:T(8,128)} %get-tuple-element.40) | copy-start | bytes 2643844
  64.6 2.3 %copy-start.5 = (f32[9,6,1,8,256]{4,0,3,1,2:T(8,128)S(1)}, f32[9,6,1,8,256]{4,0,3,1,2:T(8,128)}, u32[]{:S(2)}) copy-start(f32[9,6,1,8,256]{4,0,3,1,2:T(8,128)} %get-tuple-element.45) | copy-start | bytes 1327108
  71.1 1.0 %copy-start.15 = (f32[6,2,8,256]{3,2,1,0:T(8,128)S(1)}, f32[6,2,8,256]{3,2,1,0:T(8,128)}, u32[]{:S(2)}) copy-start(f32[6,2,8,256]{3,2,1,0:T(8,128)} %get-tuple-element.55) | copy-start | bytes 294916
  71.2 1.1 %copy-start.16 = (f32[6,2,8,256]{3,2,1,0:T(8,128)S(1)}, f32[6,2,8,256]{3,2,1,0:T(8,128)}, u32[]{:S(2)}) copy-start(f32[6,2,8,256]{3,2,1,0:T(8,128)} %get-tuple-element.56) | copy-start | bytes 294916
  (4 other events, 3.8 us)
where the time goes:
time: 85 us; the launch traced here: 84.4 us
  matrix products  36.3 us (43%)
  local copies, waits for them, and re-layouts  32.9 us (39%)
  starting transfers between devices  11 us (13%)
  other arithmetic  3.01 us (4%)
  between operations  1.23 us (1%)
    dot_general x2, matrix products, pair_face(): jnp.einsum('iltp,outp->ilou', face_layer, table, precision=lax.Precision....  18.8 us
    dot_general x6, matrix products, mix_instances(): lax.dot_general(matrix, state_now, (((1,), (0,)), ((), ())), precision=la...  17.5 us
    scatter x1, local copies, waits for them, and re-layouts, shards(): jnp.zeros_like(face_pair).at[face_pair]  8.23 us
    unnamed x70, local copies, waits for them, and re-layouts  6.34 us
    ppermute x2, starting transfers between devices, passed_along(): return lax.ppermute(block, axis, route)  5.65 us
    mul x6, local copies, waits for them, and re-layouts, apply_block(): accum_term = matrix[None, :, 0] * state_now[:, None, 0]  4.3 us
    ppermute x2, starting transfers between devices, from_behind(): return lax.ppermute(block, axis, route)  3.32 us
    ppermute x1, starting transfers between devices, partner_2(): return lax.ppermute(block, axis, route)  2.04 us
  transfers between devices with their start and end apart: 5, of which 0 were waited for; matrix products, arithmetic and copies ran while one was open for 46% of the time, Pallas kernels for 0%

commit v1 on v0

v1 whole, which is shorter than its diff:
```python
import functools
import math

import jax
import jax.numpy as jnp
from jax import lax
from jax.experimental import pallas as pl
from jax.experimental.pallas import tpu as pltpu
from jax.sharding import PartitionSpec as P

NPASS = 64
AXB = 2
NSWEEP = 3
LANES = 128
VMEM_LIMIT = 48 * 1024 * 1024


def rotations(phase_index, instances):
    harmonics = (instances - 1) // 2
    spacing = 2.0 * math.pi * jnp.arange(instances, dtype=jnp.float32) / instances
    orders = jnp.arange(1, harmonics + 1, dtype=jnp.float32)
    phases = 2.0 * math.pi * phase_index.astype(jnp.float32) / NPASS
    argument = orders[:, None] * spacing[None]
    plus = (1.0 + 2.0 * jnp.sum(jnp.cos(argument + phases[:, None]), axis=0)) / instances
    minus = (1.0 + 2.0 * jnp.sum(jnp.cos(argument - phases[:, None]), axis=0)) / instances
    return plus, minus


def spectral_weights(instances):
    harmonics = (instances - 1) // 2
    return [
        -(2.0 / instances)
        * sum(k * math.sin(2.0 * math.pi * k * d / instances) for k in range(1, harmonics + 1))
        for d in range(1, harmonics + 1)
    ]


def spectral_mix(values):
    count = len(values)
    mixed = []
    for n in range(count):
        total = None
        for d, weight in enumerate(spectral_weights(count), 1):
            term = weight * (values[(n - d) % count] - values[(n + d) % count])
            total = term if total is None else total + term
        mixed.append(total)
    return mixed


def take_lanes(tile, index):
    return jnp.take_along_axis(tile, index, axis=1, mode="promise_in_bounds")


def inverse_pairing(pairing):
    axial, span = pairing.shape
    tiles = span // LANES
    rows = axial * tiles
    row = lax.broadcasted_iota(jnp.int32, (rows, span), 0)
    wanted_row = (row % axial) * tiles + row // axial
    place = lax.broadcasted_iota(jnp.int32, (rows, span), 1)
    lane = lax.broadcasted_iota(jnp.int32, (LANES, span), 0)
    total = jnp.zeros((2 * rows, LANES), jnp.float32)
    for a in range(axial):
        target = pairing[a : a + 1]
        hit = wanted_row == target // LANES
        origin = place + a * span
        high = jnp.where(hit, origin // LANES, 0)
        low = jnp.where(hit, origin % LANES, 0)
        left = jnp.concatenate([high, low], axis=0).astype(jnp.float32).astype(jnp.bfloat16)
        right = (lane == target % LANES).astype(jnp.float32).astype(jnp.bfloat16)
        total = total + lax.dot_general(
            left, right, (((1,), (1,)), ((), ())), preferred_element_type=jnp.float32
        )
    cells = (total[:rows] * LANES + total[rows:]).astype(jnp.int32)
    return [cells[t * axial : (t + 1) * axial] for t in range(tiles)]


def far_face_kernel(place, turn, pairing, layer, *outs_and_scratch):
    *outs, index = outs_and_scratch
    instances, variables, _, _, axial, span = layer.shape
    tiles = span // LANES

    @pl.when(place[2] == 1)
    def _():
        for t, cells in enumerate(inverse_pairing(pairing[...])):
            index[t] = cells

    @pl.when(place[3] == 1)
    def _():
        for t in range(tiles):
            index[t] = pairing[:, t * LANES : (t + 1) * LANES]

    @pl.when(place[2] + place[3] == 0)
    def _():
        for t, out in enumerate(outs):
            out[...] = layer[:, :, 0, 0, :, t * LANES : (t + 1) * LANES]

    @pl.when(place[2] + place[3] > 0)
    def _():
        for t, out in enumerate(outs):
            lane = index[t] % LANES
            row = index[t] // LANES

            @pl.loop(0, variables)
            def _(v):
                picked = [jnp.zeros((axial, LANES), jnp.float32)] * instances
                for a in range(axial):
                    for s in range(tiles):
                        hit = row == a * tiles + s
                        for i in range(instances):
                            line = layer[i, v, 0, 0, a : a + 1, s * LANES : (s + 1) * LANES]
                            line = jnp.broadcast_to(line, (axial, LANES))
                            picked[i] = jnp.where(hit, take_lanes(line, lane), picked[i])
                for n in range(instances):
                    total = turn[n] * picked[0]
                    for m in range(1, instances):
                        total = total + turn[(n - m) % instances] * picked[m]
                    out[n, v] = total


def faces_kernel(place, state, axial_face, span_face):
    instances, variables, _, circ, axial, span = state.shape
    edge = jnp.where(place[4] == 0, axial - 1, 0)
    last = (place[5] == 0).astype(jnp.int32)
    lane = lax.broadcasted_iota(jnp.int32, (axial, LANES), 1)
    edge_lane = jnp.full((axial, LANES), last * (LANES - 1), jnp.int32)
    start = pl.multiple_of(last * (span - LANES), LANES)
    columns = jnp.zeros((axial, LANES), jnp.float32)
    for c in range(circ):
        for i in range(instances):
            for v in range(variables):
                k = (c * instances + i) * variables + v
                axial_face[k : k + 1] = state[i, v, 0, c, pl.ds(edge, 1), :]
                tile = take_lanes(state[i, v, 0, c, :, pl.ds(start, LANES)], edge_lane)
                columns = jnp.where(lane == k, tile, columns)
    span_face[...] = columns


def solve_tile(residual, matrix, count):
    instances, variables = count
    scale = [1.0 / matrix(v, v) for v in range(variables)]
    first = [[residual[i][v] * scale[v] for v in range(variables)] for i in range(instances)]
    update = first
    for _ in range(NSWEEP):
        later = [[None] * variables for _ in range(instances)]
        for v in range(variables):
            total = spectral_mix([update[i][v] for i in range(instances)])
            for w in range(variables):
                if w != v:
                    entry = matrix(v, w)
                    for i in range(instances):
                        total[i] = total[i] + entry * update[i][w]
            for i in range(instances):
                later[i][v] = first[i][v] - scale[v] * total[i]
        update = later
    return update


def near_kernel(place, state, source, matrix, ghost, axial_ghost, span_ghost, residual, updated):
    instances, variables, _, circ, axial, span = state.shape
    row = lax.broadcasted_iota(jnp.int32, (axial, span), 0)
    column = lax.broadcasted_iota(jnp.int32, (axial, span), 1)
    axial_row = jnp.where(place[4] == 0, axial - 1, 0)
    span_column = jnp.where(place[5] == 0, span - 1, 0)
    columns = span_ghost[...]

    @pl.loop(0, circ * variables)
    def _(step):
        c = step // variables
        v = step % variables
        near_layer = place[0] == c
        own = [state[i, v, 0, c] for i in range(instances)]
        timed = spectral_mix(own)
        for i in range(instances):
            k = (c * instances + i) * variables + v
            near = state[i, v, 0, 1 - c] + jnp.where(near_layer, ghost[i, v], 0.0)
            near = near + jnp.where(row == 0, 0.0, pltpu.roll(own[i], 1, 0))
            near = near + jnp.where(row == axial - 1, 0.0, pltpu.roll(own[i], axial - 1, 0))
            near = near + jnp.where(row == axial_row, axial_ghost[pl.ds(k, 1), :], 0.0)
            near = near + jnp.where(column == 0, 0.0, pltpu.roll(own[i], 1, 1))
            near = near + jnp.where(column == span - 1, 0.0, pltpu.roll(own[i], span - 1, 1))
            edge = take_lanes(columns, jnp.full((axial, LANES), k, jnp.int32))
            edge = jnp.concatenate([edge] * (span // LANES), axis=1)
            near = near + jnp.where(column == span_column, edge, 0.0)
            local = matrix[v, 0, 0, c] * state[i, 0, 0, c]
            for w in range(1, variables):
                local = local + matrix[v, w, 0, c] * state[i, w, 0, c]
            residual[i, v, 0, c] = source[i, v, 0, c] - (local - near + timed[i])

    c = place[0]

    @pl.loop(0, span // LANES)
    def _(t):
        lanes = pl.ds(pl.multiple_of(t * LANES, LANES), LANES)
        right = [
            [residual[i, v, 0, c, :, lanes] for v in range(variables)] for i in range(instances)
        ]
        update = solve_tile(
            right, lambda v, w: matrix[v, w, 0, c, :, lanes], (instances, variables)
        )
        for i in range(instances):
            for v in range(variables):
                updated[i, v, 0, c, :, lanes] = state[i, v, 0, c, :, lanes] + update[i][v]


def far_kernel(place, partial, _, state, matrix, ghost, residual, updated):
    instances, variables = ghost.shape[:2]
    right = []
    for i in range(instances):
        right.append([])
        for v in range(variables):
            value = partial[i, v, 0, 0] + ghost[i, v]
            residual[i, v, 0, 0] = value
            right[i].append(value)
    update = solve_tile(right, lambda v, w: matrix[v, w, 0, 0], (instances, variables))
    for i in range(instances):
        for v in range(variables):
            updated[i, v, 0, 0] = state[i, v, 0, 0] + update[i][v]


def whole(shape, *, space=pltpu.VMEM):
    zeros = (0,) * len(shape)
    return pl.BlockSpec(shape, lambda step, place: zeros, memory_space=space)


def call(kernel, name, operands, in_specs, outs, out_specs, scratch=(), aliases=None):
    return pl.pallas_call(
        kernel,
        name=name,
        grid_spec=pltpu.PrefetchScalarGridSpec(
            num_scalar_prefetch=1,
            grid=(1,),
            in_specs=in_specs,
            out_specs=out_specs,
            scratch_shapes=scratch,
        ),
        out_shape=outs,
        input_output_aliases=aliases or {},
        compiler_params=pltpu.CompilerParams(vmem_limit_bytes=VMEM_LIMIT),
    )(*operands)


def shards(state, source, block_matrix, phase_index, face_pair):
    instances, variables, _, circ, axial, span = state.shape
    tiles = span // LANES
    blocks = lax.axis_size("blocks")
    rings = blocks // AXB
    position = lax.axis_index("blocks")
    circ_place = position // AXB
    even = circ_place % 2 == 0
    near_layer = jnp.where(even, circ - 1, 0)
    far_layer = jnp.where(even, 0, circ - 1)
    at_first = circ_place == 0
    at_last = circ_place == rings - 1
    place = jnp.stack(
        [
            near_layer,
            far_layer,
            at_first,
            at_last,
            position % AXB,
            lax.axis_index("span"),
        ]
    ).astype(jnp.int32)

    def ring_partner(block, first):
        hop = 1 if block // AXB % 2 == first else -1
        return (block // AXB + hop) % rings * AXB + block % AXB

    near_route = [(b, ring_partner(b, 0)) for b in range(blocks)]
    far_route = [(b, ring_partner(b, 1)) for b in range(blocks)]
    axial_route = [(b, b ^ 1) for b in range(blocks)]

    near_face = lax.dynamic_slice_in_dim(state, near_layer, 1, 3)[:, :, 0, 0]
    near_ghost = lax.ppermute(near_face, "blocks", near_route)

    plus, minus = rotations(phase_index, instances)
    turn = jnp.where(at_first, plus, minus)
    pairing = face_pair.reshape(axial, span)
    layer_shape = (instances, variables, 1, 1, axial, span)
    chunk = jax.ShapeDtypeStruct((instances, variables, axial, LANES), jnp.float32)
    far_faces = call(
        far_face_kernel,
        "far_face",
        (place, turn, pairing, state),
        [
            pl.BlockSpec(memory_space=pltpu.SMEM),
            whole((axial, span)),
            pl.BlockSpec(layer_shape, lambda step, place: (0, 0, 0, place[1], 0, 0)),
        ],
        [chunk] * tiles,
        [whole(chunk.shape)] * tiles,
        [pltpu.VMEM((tiles, axial, LANES), jnp.int32)],
    )
    far_ghosts = [lax.ppermute(face, "blocks", far_route) for face in far_faces]

    faces = circ * instances * variables
    axial_face, span_face = call(
        faces_kernel,
        "faces",
        (place, state),
        [whole(state.shape)],
        [
            jax.ShapeDtypeStruct((faces, span), jnp.float32),
            jax.ShapeDtypeStruct((axial, LANES), jnp.float32),
        ],
        [whole((faces, span)), whole((axial, LANES))],
    )
    axial_ghost = lax.ppermute(axial_face, "blocks", axial_route)
    span_ghost = lax.ppermute(span_face, "span", [(0, 1), (1, 0)])

    out = jax.ShapeDtypeStruct(state.shape, jnp.float32)
    residual, updated = call(
        near_kernel,
        "near",
        (place, state, source, block_matrix, near_ghost, axial_ghost, span_ghost),
        [
            whole(state.shape),
            whole(source.shape),
            whole(block_matrix.shape),
            whole(near_ghost.shape),
            whole(axial_ghost.shape),
            whole(span_ghost.shape),
        ],
        [out, out],
        [whole(out.shape), whole(out.shape)],
    )

    for t, ghost in enumerate(far_ghosts):
        def part(lead):
            return pl.BlockSpec(
                (lead, variables, 1, 1, axial, LANES),
                lambda step, place: (0, 0, 0, place[1], 0, t),
            )

        residual, updated = call(
            far_kernel,
            "far",
            (place, residual, updated, state, block_matrix, ghost),
            [
                part(instances),
                pl.BlockSpec(memory_space=pl.ANY),
                part(instances),
                part(variables),
                whole(ghost.shape),
            ],
            [out, out],
            [part(instances), part(instances)],
            aliases={1: 0, 2: 1},
        )
    return updated, residual


def solution(mesh):
    placed = P(None, None, ("groups", "blocks"), None, None, "span")
    return jax.shard_map(
        shards,
        mesh=mesh,
        in_specs=(placed, placed, placed, P("groups"), P()),
        out_specs=(placed, placed),
        check_vma=False,
    )
```

time: 85 us -> 33.4 us (0.39)
  the two profiles are of different devices: /device:TPU:1 before, /device:TPU:24 now
where the time goes in v1:
time: 33.4 us; the launch traced here: 33.1 us
  Pallas kernels  14.5 us (43%)
  waiting for transfers between devices  9.94 us (30%)
  starting transfers between devices  5.96 us (18%)
  local copies, waits for them, and re-layouts  1.9 us (6%)
  between operations  0.73 us (2%)
    pallas_call x5, Pallas kernels, call(): pl.pallas_call(kernel, name=name, grid_spec=pltpu.PrefetchScalarGridSpec(...  14.5 us
    ppermute x1, waiting for transfers between devices, shards(): near_ghost = lax.ppermute(near_face, 'blocks', near_route)  6.63 us
    ppermute x2, starting transfers between devices, shards(): far_ghosts = [lax.ppermute(face, 'blocks', far_route) for face in far_faces]  3.89 us
    ppermute x1, waiting for transfers between devices, shards(): axial_ghost = lax.ppermute(axial_face, 'blocks', axial_route)  2.13 us
    ppermute x1, starting transfers between devices, shards(): axial_ghost = lax.ppermute(axial_face, 'blocks', axial_route)  1.56 us
    ppermute x1, waiting for transfers between devices, shards(): span_ghost = lax.ppermute(span_face, 'span', [(0, 1), (1, 0)])  1.16 us
    squeeze x1, local copies, waits for them, and re-layouts, shards(): near_face = lax.dynamic_slice_in_dim(state, near_layer, 1, 3)[:, :, 0, 0]  1.12 us
    unnamed x10, local copies, waits for them, and re-layouts  0.7 us
  transfers between devices with their start and end apart: 5, of which 3 were waited for; matrix products, arithmetic and copies ran while one was open for 1% of the time, Pallas kernels for 35%

profile of v1, /device:TPU:24, one launch (start us, length us, event | category | flops | bytes accessed | tf_op | source)
XLA Modules:
  0.0 33.1 jit_solution(18286792913710952617)
XLA Ops:
  0.6 0.0 copy-start
  0.7 1.1 %dynamic-slice_bitcast_fusion = f32[9,6,8,256]{3,2,1,0:T(8,128)S(1)} fusion(f32[9,6,1,2,8,256]{5,4,3,2,1,0:T(8,128)} %state.7, s32[]{:T(128)} %select_n.33), kind=kLoop, calls=%fused_computation | loop fusion | bytes 884740 | tf_op jit(solution)/shard_map/squeeze | solution.py:274
  1.8 0.5 %collective-permute-start = (f32[9,6,8,256]{3,2,1,0:T(8,128)S(1)}, f32[9,6,8,256]{3,2,1,0:T(8,128)S(1)}, u32[]{:S(2)}, u32[]{:S(2)}) collective-permute-start(f32[9,6,8,256]{3,2,1,0:T(8,128)S(1)} %dynamic-slice_bitcast_fusion), channel_id=1, source_target_pairs={{0,4},{2,6},{4,0},{6,2},{8,12},{10,14},{12,8},{14,10},{1,5},{3,7},... | collective-permute-start | bytes 1327112 | tf_op jit(solution)/shard_map/ppermute | solution.py:275
  2.3 0.0 copy-start.3
  2.3 0.0 copy-start.4
  2.3 0.7 %copy-done.4 = s32[4]{0:T(128)S(1)} copy-done((s32[4]{0:T(128)S(1)}, s32[4]{0:T(128)}, u32[]{:S(2)}) %copy-start.4) | copy-done | bytes 40
  3.0 0.0 copy-done.3
  3.0 0.1 fusion.1
  3.1 0.1 stack.35.place
  3.2 0.0 copy-done
  3.2 0.0 copy-start.2
  3.3 3.9 %far_face.1 = (f32[9,6,8,128]{3,2,1,0:T(8,128)S(1)}, f32[9,6,8,128]{3,2,1,0:T(8,128)S(1)}) custom-call(s32[6]{0:T(128)S(1)} %stack.35.place, f32[9]{0:T(128)S(1)} %broadcast_select_fusion.turn, s32[8,256]{1,0:T(8,128)S(1)} %reshape.16.pairing, f32[9,6,1,2,8,256]{5,4,3,2,1,0:T(8,128)S(1)} %copy-done), custom_call_target="tpu_custom_call" | custom-call | tf_op jit(solution)/shard_map/far_face/pallas_call | solution.py:227
  7.1 0.0 copy-start.1
  7.1 1.7 %collective-permute-start.3 = (f32[9,6,8,128]{3,2,1,0:T(8,128)S(1)}, f32[9,6,8,128]{3,2,1,0:T(8,128)S(1)}, u32[]{:S(2)}, u32[]{:S(2)}) collective-permute-start(f32[9,6,8,128]{3,2,1,0:T(8,128)S(1)} %get-tuple-element.16), channel_id=1, source_target_pairs={{0,12},{2,14},{4,8},{6,10},{8,4},{10,6},{12,0},{14,2},{1,13},{3,15... | collective-permute-start | bytes 663560 | tf_op jit(solution)/shard_map/ppermute | solution.py:295
  8.8 2.2 %collective-permute-start.4 = (f32[9,6,8,128]{3,2,1,0:T(8,128)S(1)}, f32[9,6,8,128]{3,2,1,0:T(8,128)S(1)}, u32[]{:S(2)}, u32[]{:S(2)}) collective-permute-start(f32[9,6,8,128]{3,2,1,0:T(8,128)S(1)} %get-tuple-element.19), channel_id=1, source_target_pairs={{0,12},{2,14},{4,8},{6,10},{8,4},{10,6},{12,0},{14,2},{1,13},{3,15... | collective-permute-start | bytes 663560 | tf_op jit(solution)/shard_map/ppermute | solution.py:295
  11.0 0.7 %faces.1 = (f32[108,256]{1,0:T(8,128)S(1)}, f32[8,128]{1,0:T(8,128)S(1)}) custom-call(s32[6]{0:T(128)S(1)} %stack.35.place, f32[9,6,1,2,8,256]{5,4,3,2,1,0:T(8,128)S(1)} %copy-done), custom_call_target="tpu_custom_call" | custom-call | tf_op jit(solution)/shard_map/faces/pallas_call | solution.py:227
  11.8 1.6 %collective-permute-start.1 = (f32[108,256]{1,0:T(8,128)S(1)}, f32[108,256]{1,0:T(8,128)S(1)}, u32[]{:S(2)}, u32[]{:S(2)}) collective-permute-start(f32[108,256]{1,0:T(8,128)S(1)} %get-tuple-element.12), channel_id=1, source_target_pairs={{0,2},{2,0},{4,6},{6,4},{8,10},{10,8},{12,14},{14,12},{1,3},{3,1},... | collective-permute-start | bytes 331784 | tf_op jit(solution)/shard_map/ppermute | solution.py:309
  13.3 0.0 collective-permute-start.2
  13.3 1.2 %collective-permute-done.2.span_ghost = f32[8,128]{1,0:T(8,128)S(1)} collective-permute-done((f32[8,128]{1,0:T(8,128)S(1)}, f32[8,128]{1,0:T(8,128)S(1)}, u32[]{:S(2)}, u32[]{:S(2)}) %collective-permute-start.2) | collective-permute-done | bytes 4128 | tf_op jit(solution)/shard_map/ppermute | solution.py:310
  14.5 2.1 %collective-permute-done.1.axial_ghost = f32[108,256]{1,0:T(8,128)S(1)} collective-permute-done((f32[108,256]{1,0:T(8,128)S(1)}, f32[108,256]{1,0:T(8,128)S(1)}, u32[]{:S(2)}, u32[]{:S(2)}) %collective-permute-start.1) | collective-permute-done | bytes 110624 | tf_op jit(solution)/shard_map/ppermute | solution.py:309
  16.6 6.6 %collective-permute-done.ghost = f32[9,6,8,256]{3,2,1,0:T(8,128)S(1)} collective-permute-done((f32[9,6,8,256]{3,2,1,0:T(8,128)S(1)}, f32[9,6,8,256]{3,2,1,0:T(8,128)S(1)}, u32[]{:S(2)}, u32[]{:S(2)}) %collective-permute-start) | collective-permute-done | bytes 442400 | tf_op jit(solution)/shard_map/ppermute | solution.py:275
  23.2 0.0 copy-done.2
  23.3 0.0 copy-done.1
  23.3 4.4 %near.1 = (f32[9,6,1,2,8,256]{5,4,3,2,1,0:T(8,128)}, f32[9,6,1,2,8,256]{5,4,3,2,1,0:T(8,128)}) custom-call(s32[6]{0:T(128)S(1)} %stack.35.place, f32[9,6,1,2,8,256]{5,4,3,2,1,0:T(8,128)S(1)} %copy-done, f32[9,6,1,2,8,256]{5,4,3,2,1,0:T(8,128)S(1)} %copy-done.2, f32[6,6,1,2,8,256]{5,4,3,2,1,0:T(8,128)S(1)} %copy-done.1, ...), custom_call_target="tpu_custom_call" | custom-call | tf_op jit(solution)/shard_map/near/pallas_call | solution.py:227
  27.6 0.0 collective-permute-done.3.ghost
  27.6 2.7 %far.2 = (f32[9,6,1,2,8,256]{5,4,3,2,1,0:T(8,128)}, f32[9,6,1,2,8,256]{5,4,3,2,1,0:T(8,128)}) custom-call(s32[6]{0:T(128)S(1)} %stack.35.place, f32[9,6,1,2,8,256]{5,4,3,2,1,0:T(8,128)} %get-tuple-element.14.partial, f32[9,6,1,2,8,256]{5,4,3,2,1,0:T(8,128)} %get-tuple-element.15._, ...), custom_call_target="tpu_custom_call", output_to_operand_aliasing={{0}: (1, {}), {1}: (2, {})} | custom-call | tf_op jit(solution)/shard_map/far/pallas_call | solution.py:227
  30.4 0.0 collective-permute-done.4.ghost
  30.4 2.7 %far.3 = (f32[9,6,1,2,8,256]{5,4,3,2,1,0:T(8,128)}, f32[9,6,1,2,8,256]{5,4,3,2,1,0:T(8,128)}) custom-call(s32[6]{0:T(128)S(1)} %stack.35.place, f32[9,6,1,2,8,256]{5,4,3,2,1,0:T(8,128)} %get-tuple-element.17.partial, f32[9,6,1,2,8,256]{5,4,3,2,1,0:T(8,128)} %get-tuple-element.18._, ...), custom_call_target="tpu_custom_call", output_to_operand_aliasing={{0}: (1, {}), {1}: (2, {})} | custom-call | tf_op jit(solution)/shard_map/far/pallas_call | solution.py:227
  (4 shorter events, 0.0 us)
Async XLA Ops:
  0.6 2.6 %copy-start = (f32[9,6,1,2,8,256]{5,4,3,2,1,0:T(8,128)S(1)}, f32[9,6,1,2,8,256]{5,4,3,2,1,0:T(8,128)}, u32[]{:S(2)}) copy-start(f32[9,6,1,2,8,256]{5,4,3,2,1,0:T(8,128)} %state.7) | copy-start | bytes 2654212
  1.8 21.5 %collective-permute-start = (f32[9,6,8,256]{3,2,1,0:T(8,128)S(1)}, f32[9,6,8,256]{3,2,1,0:T(8,128)S(1)}, u32[]{:S(2)}, u32[]{:S(2)}) collective-permute-start(f32[9,6,8,256]{3,2,1,0:T(8,128)S(1)} %dynamic-slice_bitcast_fusion), channel_id=1, source_target_pairs={{0,4},{2,6},{4,0},{6,2},{8,12},{10,14},{12,8},{14,10},{1,5},{3,7},... | collective-permute-start | bytes 1327112 | tf_op jit(solution)/shard_map/ppermute | solution.py:275
  2.3 0.7 %copy-start.3 = (s32[2048]{0:T(1024)S(1)}, s32[2048]{0:T(1024)}, u32[]{:S(2)}) copy-start(s32[2048]{0:T(1024)} %param.9) | copy-start | bytes 24580
  2.3 0.7 %copy-start.4 = (s32[4]{0:T(128)S(1)}, s32[4]{0:T(128)}, u32[]{:S(2)}) copy-start(s32[4]{0:T(128)} %param.8) | copy-start | bytes 52
  3.2 20.0 %copy-start.2 = (f32[9,6,1,2,8,256]{5,4,3,2,1,0:T(8,128)S(1)}, f32[9,6,1,2,8,256]{5,4,3,2,1,0:T(8,128)}, u32[]{:S(2)}) copy-start(f32[9,6,1,2,8,256]{5,4,3,2,1,0:T(8,128)} %source.1) | copy-start | bytes 2654212
  7.1 16.1 %copy-start.1 = (f32[6,6,1,2,8,256]{5,4,3,2,1,0:T(8,128)S(1)}, f32[6,6,1,2,8,256]{5,4,3,2,1,0:T(8,128)}, u32[]{:S(2)}) copy-start(f32[6,6,1,2,8,256]{5,4,3,2,1,0:T(8,128)} %matrix.5) | copy-start | bytes 1769476
  7.1 20.5 %collective-permute-start.3 = (f32[9,6,8,128]{3,2,1,0:T(8,128)S(1)}, f32[9,6,8,128]{3,2,1,0:T(8,128)S(1)}, u32[]{:S(2)}, u32[]{:S(2)}) collective-permute-start(f32[9,6,8,128]{3,2,1,0:T(8,128)S(1)} %get-tuple-element.16), channel_id=1, source_target_pairs={{0,12},{2,14},{4,8},{6,10},{8,4},{10,6},{12,0},{14,2},{1,13},{3,15... | collective-permute-start | bytes 663560 | tf_op jit(solution)/shard_map/ppermute | solution.py:295
  8.8 21.6 %collective-permute-start.4 = (f32[9,6,8,128]{3,2,1,0:T(8,128)S(1)}, f32[9,6,8,128]{3,2,1,0:T(8,128)S(1)}, u32[]{:S(2)}, u32[]{:S(2)}) collective-permute-start(f32[9,6,8,128]{3,2,1,0:T(8,128)S(1)} %get-tuple-element.19), channel_id=1, source_target_pairs={{0,12},{2,14},{4,8},{6,10},{8,4},{10,6},{12,0},{14,2},{1,13},{3,15... | collective-permute-start | bytes 663560 | tf_op jit(solution)/shard_map/ppermute | solution.py:295
  11.8 4.9 %collective-permute-start.1 = (f32[108,256]{1,0:T(8,128)S(1)}, f32[108,256]{1,0:T(8,128)S(1)}, u32[]{:S(2)}, u32[]{:S(2)}) collective-permute-start(f32[108,256]{1,0:T(8,128)S(1)} %get-tuple-element.12), channel_id=1, source_target_pairs={{0,2},{2,0},{4,6},{6,4},{8,10},{10,8},{12,14},{14,12},{1,3},{3,1},... | collective-permute-start | bytes 331784 | tf_op jit(solution)/shard_map/ppermute | solution.py:309
  13.3 1.2 %collective-permute-start.2 = (f32[8,128]{1,0:T(8,128)S(1)}, f32[8,128]{1,0:T(8,128)S(1)}, u32[]{:S(2)}, u32[]{:S(2)}) collective-permute-start(f32[8,128]{1,0:T(8,128)S(1)} %get-tuple-element.13), channel_id=1, source_target_pairs={{0,1},{1,0},{2,3},{3,2},{4,5},{5,4},{6,7},{7,6},{8,9},{9,8},{10,11... | collective-permute-start | bytes 12296 | tf_op jit(solution)/shard_map/ppermute | solution.py:310

commit v2 on v1

v2 whole, which is shorter than its diff:
```python
import functools
import math

import jax
import jax.numpy as jnp
from jax import lax
from jax.experimental import pallas as pl
from jax.experimental.pallas import tpu as pltpu
from jax.sharding import PartitionSpec as P

NPASS = 64
AXB = 2
NSWEEP = 3
LANES = 128
VMEM_LIMIT = 48 * 1024 * 1024


def rotations(phase_index, instances):
    harmonics = (instances - 1) // 2
    spacing = 2.0 * math.pi * jnp.arange(instances, dtype=jnp.float32) / instances
    orders = jnp.arange(1, harmonics + 1, dtype=jnp.float32)
    phases = 2.0 * math.pi * phase_index.astype(jnp.float32) / NPASS
    argument = orders[:, None] * spacing[None]
    plus = (1.0 + 2.0 * jnp.sum(jnp.cos(argument + phases[:, None]), axis=0)) / instances
    minus = (1.0 + 2.0 * jnp.sum(jnp.cos(argument - phases[:, None]), axis=0)) / instances
    return plus, minus


def spectral_weights(instances):
    harmonics = (instances - 1) // 2
    return [
        -(2.0 / instances)
        * sum(k * math.sin(2.0 * math.pi * k * d / instances) for k in range(1, harmonics + 1))
        for d in range(1, harmonics + 1)
    ]


def spectral_mix(values):
    count = len(values)
    mixed = []
    for n in range(count):
        total = None
        for d, weight in enumerate(spectral_weights(count), 1):
            term = weight * (values[(n - d) % count] - values[(n + d) % count])
            total = term if total is None else total + term
        mixed.append(total)
    return mixed


def take_lanes(tile, index):
    return jnp.take_along_axis(tile, index, axis=1, mode="promise_in_bounds")


def inverse_pairing(pairing):
    axial, span = pairing.shape
    tiles = span // LANES
    rows = axial * tiles
    row = lax.broadcasted_iota(jnp.int32, (rows, span), 0)
    wanted_row = (row % axial) * tiles + row // axial
    place = lax.broadcasted_iota(jnp.int32, (rows, span), 1)
    lane = lax.broadcasted_iota(jnp.int32, (LANES, span), 0)
    total = jnp.zeros((2 * rows, LANES), jnp.float32)
    for a in range(axial):
        target = pairing[a : a + 1]
        hit = wanted_row == target // LANES
        origin = place + a * span
        high = jnp.where(hit, origin // LANES, 0)
        low = jnp.where(hit, origin % LANES, 0)
        left = jnp.concatenate([high, low], axis=0).astype(jnp.float32).astype(jnp.bfloat16)
        right = (lane == target % LANES).astype(jnp.float32).astype(jnp.bfloat16)
        total = total + lax.dot_general(
            left, right, (((1,), (1,)), ((), ())), preferred_element_type=jnp.float32
        )
    cells = (total[:rows] * LANES + total[rows:]).astype(jnp.int32)
    return [cells[t * axial : (t + 1) * axial] for t in range(tiles)]


def places():
    rings = lax.axis_size("blocks") // AXB
    position = lax.axis_index("blocks")
    ring = position // AXB
    near = 1 - ring % 2
    return near, 1 - near, ring == 0, ring == rings - 1, position % AXB, lax.axis_index("span")


def split_kernel(state, far_face, near_face, sems):
    near, far = places()[:2]
    copies = [
        pltpu.make_async_copy(state.at[:, :, 0, far], far_face, sems.at[0]),
        pltpu.make_async_copy(state.at[:, :, 0, near], near_face, sems.at[1]),
    ]
    for copy in copies:
        copy.start()
    for copy in copies:
        copy.wait()


def paired_kernel(turn, pairing, state, _, *outs_and_scratch):
    *outs, index = outs_and_scratch
    instances, variables, _, _, axial, span = state.shape
    tiles = span // LANES
    _, far, first, last, _, _ = places()

    @pl.when(first)
    def _():
        for t, cells in enumerate(inverse_pairing(pairing[...])):
            index[t] = cells

    @pl.when(last)
    def _():
        for t in range(tiles):
            index[t] = pairing[:, t * LANES : (t + 1) * LANES]

    @pl.when(first | last)
    def _():
        for t, out in enumerate(outs):
            lane = index[t] % LANES
            row = index[t] // LANES

            @pl.loop(0, variables)
            def _(v):
                picked = [jnp.zeros((axial, LANES), jnp.float32)] * instances
                for a in range(axial):
                    for s in range(tiles):
                        hit = row == a * tiles + s
                        for i in range(instances):
                            line = state[i, v, 0, far, a : a + 1, s * LANES : (s + 1) * LANES]
                            line = jnp.broadcast_to(line, (axial, LANES))
                            picked[i] = jnp.where(hit, take_lanes(line, lane), picked[i])
                for n in range(instances):
                    total = turn[n] * picked[0]
                    for m in range(1, instances):
                        total = total + turn[(n - m) % instances] * picked[m]
                    out[n, v] = total


def faces_kernel(state, axial_face, span_face):
    instances, variables, _, circ, axial, span = state.shape
    _, _, _, _, axial_place, span_place = places()
    edge = jnp.where(axial_place == 0, axial - 1, 0)
    last = (span_place == 0).astype(jnp.int32)
    lane = lax.broadcasted_iota(jnp.int32, (axial, LANES), 1)
    edge_lane = jnp.full((axial, LANES), last * (LANES - 1), jnp.int32)
    start = pl.multiple_of(last * (span - LANES), LANES)
    columns = jnp.zeros((axial, LANES), jnp.float32)
    for c in range(circ):
        for i in range(instances):
            for v in range(variables):
                k = (c * instances + i) * variables + v
                axial_face[k : k + 1] = state[i, v, 0, c, pl.ds(edge, 1), :]
                tile = take_lanes(state[i, v, 0, c, :, pl.ds(start, LANES)], edge_lane)
                columns = jnp.where(lane == k, tile, columns)
    span_face[...] = columns


def solve_tile(residual, matrix, count):
    instances, variables = count
    scale = [1.0 / matrix(v, v) for v in range(variables)]
    first = [[residual[i][v] * scale[v] for v in range(variables)] for i in range(instances)]
    update = first
    for _ in range(NSWEEP):
        later = [[None] * variables for _ in range(instances)]
        for v in range(variables):
            total = spectral_mix([update[i][v] for i in range(instances)])
            for w in range(variables):
                if w != v:
                    entry = matrix(v, w)
                    for i in range(instances):
                        total[i] = total[i] + entry * update[i][w]
            for i in range(instances):
                later[i][v] = first[i][v] - scale[v] * total[i]
        update = later
    return update


def base_kernel(state, source, matrix, axial_ghost, span_ghost, partial):
    instances, variables, _, circ, axial, span = state.shape
    _, _, _, _, axial_place, span_place = places()
    row = lax.broadcasted_iota(jnp.int32, (axial, span), 0)
    column = lax.broadcasted_iota(jnp.int32, (axial, span), 1)
    axial_row = jnp.where(axial_place == 0, axial - 1, 0)
    span_column = jnp.where(span_place == 0, span - 1, 0)
    columns = span_ghost[...]

    @pl.loop(0, circ * variables)
    def _(step):
        c = step // variables
        v = step % variables
        own = [state[i, v, 0, c] for i in range(instances)]
        timed = spectral_mix(own)
        for i in range(instances):
            k = (c * instances + i) * variables + v
            near = state[i, v, 0, 1 - c]
            near = near + jnp.where(row == 0, 0.0, pltpu.roll(own[i], 1, 0))
            near = near + jnp.where(row == axial - 1, 0.0, pltpu.roll(own[i], axial - 1, 0))
            near = near + jnp.where(row == axial_row, axial_ghost[pl.ds(k, 1), :], 0.0)
            near = near + jnp.where(column == 0, 0.0, pltpu.roll(own[i], 1, 1))
            near = near + jnp.where(column == span - 1, 0.0, pltpu.roll(own[i], span - 1, 1))
            edge = take_lanes(columns, jnp.full((axial, LANES), k, jnp.int32))
            edge = jnp.concatenate([edge] * (span // LANES), axis=1)
            near = near + jnp.where(column == span_column, edge, 0.0)
            local = matrix[v, 0, 0, c] * state[i, 0, 0, c]
            for w in range(1, variables):
                local = local + matrix[v, w, 0, c] * state[i, w, 0, c]
            partial[i, v, c] = source[i, v, 0, c] - (local - near + timed[i])


def finish_tile(c, t, ghost, partial, state, matrix, residual, updated, buffers, sems):
    instances, variables, _, axial, _ = partial.shape
    lanes = slice(t * LANES, (t + 1) * LANES)
    copies = [
        pltpu.make_async_copy(buffers.at[n], whole.at[:, :, 0, c, :, lanes], sems.at[n])
        for n, whole in enumerate((residual, updated))
    ]
    right = []
    for i in range(instances):
        right.append([])
        for v in range(variables):
            value = partial[i, v, c, :, lanes] + ghost(i, v, lanes)
            buffers[0, i, v] = value
            right[i].append(value)
    copies[0].start()
    update = solve_tile(right, lambda v, w: matrix[v, w, 0, c, :, lanes], (instances, variables))
    for i in range(instances):
        for v in range(variables):
            buffers[1, i, v] = state[i, v, 0, c, :, lanes] + update[i][v]
    copies[1].start()
    return copies


def near_kernel(partial, state, matrix, ghost, residual, updated, buffers, sems):
    copies = []
    for t in range(partial.shape[-1] // LANES):
        copies += finish_tile(
            places()[0],
            t,
            lambda i, v, lanes: ghost[i, v, :, lanes],
            partial,
            state,
            matrix,
            residual,
            updated,
            buffers.at[t],
            sems.at[t],
        )
    for copy in copies:
        copy.wait()


def far_kernel(t, partial, state, matrix, ghost, paired, _, __, residual, updated, buffers, sems):
    _, far, first, last, _, _ = places()
    copies = finish_tile(
        far,
        t,
        lambda i, v, lanes: jnp.where(first | last, paired[i, v], ghost[i, v, :, lanes]),
        partial,
        state,
        matrix,
        residual,
        updated,
        buffers,
        sems,
    )
    for copy in copies:
        copy.wait()


def call(kernel, name, operands, outs, in_vmem=(), out_vmem=True, scratch=(), aliases=None):
    vmem = pl.BlockSpec(memory_space=pltpu.VMEM)
    anywhere = pl.BlockSpec(memory_space=pl.ANY)
    smem = pl.BlockSpec(memory_space=pltpu.SMEM)
    kinds = {"v": vmem, "a": anywhere, "s": smem}
    return pl.pallas_call(
        kernel,
        name=name,
        in_specs=[kinds[k] for k in in_vmem],
        out_specs=[vmem if out_vmem else anywhere] * len(outs),
        out_shape=outs,
        scratch_shapes=scratch,
        input_output_aliases=aliases or {},
        compiler_params=pltpu.CompilerParams(vmem_limit_bytes=VMEM_LIMIT),
    )(*operands)


def shards(state, source, block_matrix, phase_index, face_pair):
    instances, variables, _, circ, axial, span = state.shape
    tiles = span // LANES
    blocks = lax.axis_size("blocks")
    rings = blocks // AXB

    def array(*shape):
        return jax.ShapeDtypeStruct(shape, jnp.float32)

    def across(block):
        return block ^ 1

    def ring_partner(block, first):
        hop = 1 if block // AXB % 2 == first else -1
        return (block // AXB + hop) % rings * AXB + block % AXB

    def at_end(block):
        return block // AXB in (0, rings - 1)

    every = range(blocks)
    near_route = [(b, ring_partner(b, 0)) for b in every]
    middle_route = [(b, across(b) if at_end(b) else ring_partner(b, 1)) for b in every]
    paired_route = [(b, ring_partner(b, 1) if at_end(b) else across(b)) for b in every]
    axial_route = [(b, across(b)) for b in every]

    layer = array(instances, variables, axial, span)
    far_face, near_face = call(
        split_kernel,
        "split",
        (state,),
        [layer, layer],
        "a",
        scratch=[pltpu.SemaphoreType.DMA((2,))],
    )
    middle_ghost = lax.ppermute(far_face, "blocks", middle_route)
    near_ghost = lax.ppermute(near_face, "blocks", near_route)

    faces = circ * instances * variables
    axial_face, span_face = call(
        faces_kernel, "faces", (state,), [array(faces, span), array(axial, LANES)], "v"
    )
    axial_ghost = lax.ppermute(axial_face, "blocks", axial_route)
    span_ghost = lax.ppermute(span_face, "span", [(0, 1), (1, 0)])

    plus, minus = rotations(phase_index, instances)
    turn = jnp.where(lax.axis_index("blocks") < AXB, plus, minus)
    paired_faces = call(
        paired_kernel,
        "paired",
        (turn, face_pair.reshape(axial, span), state, span_face),
        [array(instances, variables, axial, LANES)] * tiles,
        "svva",
        scratch=[pltpu.VMEM((tiles, axial, LANES), jnp.int32)],
    )
    paired_ghosts = [lax.ppermute(face, "blocks", paired_route) for face in paired_faces]

    (partial,) = call(
        base_kernel,
        "base",
        (state, source, block_matrix, axial_ghost, span_ghost),
        [array(instances, variables, circ, axial, span)],
        "vvvvv",
    )

    out = array(*state.shape)
    tile = (2, instances, variables, axial, LANES)
    residual, updated = call(
        near_kernel,
        "near",
        (partial, state, block_matrix, near_ghost),
        [out, out],
        "vvvv",
        out_vmem=False,
        scratch=[pltpu.VMEM((tiles,) + tile, jnp.float32), pltpu.SemaphoreType.DMA((tiles, 2))],
    )
    for t, ghost in enumerate(paired_ghosts):
        residual, updated = call(
            functools.partial(far_kernel, t),
            "far",
            (partial, state, block_matrix, middle_ghost, ghost, residual, updated),
            [out, out],
            "vvvvvaa",
            out_vmem=False,
            scratch=[pltpu.VMEM(tile, jnp.float32), pltpu.SemaphoreType.DMA((2,))],
            aliases={5: 0, 6: 1},
        )
    return updated, residual


def solution(mesh):
    placed = P(None, None, ("groups", "blocks"), None, None, "span")
    return jax.shard_map(
        shards,
        mesh=mesh,
        in_specs=(placed, placed, placed, P("groups"), P()),
        out_specs=(placed, placed),
        check_vma=False,
    )
```

time: 33.4 us -> 30.5 us (0.913)
  the two profiles are of different devices: /device:TPU:24 before, /device:TPU:0 now
where the time goes in v2:
time: 30.5 us; the launch traced here: 30.3 us
  Pallas kernels  11.3 us (37%)
  starting transfers between devices  10 us (33%)
  waiting for transfers between devices  6.48 us (21%)
  local copies, waits for them, and re-layouts  1.6 us (5%)
  between operations  0.75 us (2%)
    pallas_call x7, Pallas kernels, call(): pl.pallas_call(kernel, name=name, in_specs=[kinds[k] for k in in_vmem], o...  11.3 us
    ppermute x2, starting transfers between devices, shards(): lax.ppermute(face, 'blocks', paired_route)  3.89 us
    ppermute x1, waiting for transfers between devices, shards(): axial_ghost = lax.ppermute(axial_face, 'blocks', axial_route)  3.73 us
    ppermute x1, starting transfers between devices, shards(): middle_ghost = lax.ppermute(far_face, 'blocks', middle_route)  3 us
    ppermute x1, starting transfers between devices, shards(): near_ghost = lax.ppermute(near_face, 'blocks', near_route)  1.66 us
    unnamed x12, local copies, waits for them, and re-layouts  1.59 us
    ppermute x2, waiting for transfers between devices, shards(): lax.ppermute(face, 'blocks', paired_route)  1.58 us
    ppermute x1, starting transfers between devices, shards(): axial_ghost = lax.ppermute(axial_face, 'blocks', axial_route)  1.49 us
  transfers between devices with their start and end apart: 6, of which 3 were waited for; matrix products, arithmetic and copies ran while one was open for 1% of the time, Pallas kernels for 30%

profile of v2, /device:TPU:0, one launch (start us, length us, event | category | flops | bytes accessed | tf_op | source)
XLA Modules:
  0.0 30.3 jit_solution(11425790004344112106)
XLA Ops:
  0.6 0.0 copy-start
  0.6 1.2 %copy-done = f32[9,6,1,2,8,256]{5,4,3,2,1,0:T(8,128)S(1)} copy-done((f32[9,6,1,2,8,256]{5,4,3,2,1,0:T(8,128)S(1)}, f32[9,6,1,2,8,256]{5,4,3,2,1,0:T(8,128)}, u32[]{:S(2)}) %copy-start) | copy-done | bytes 884760
  1.8 0.0 copy-start.5
  1.8 0.0 copy-start.1
  1.8 1.0 %split.1 = (f32[9,6,8,256]{3,2,1,0:T(8,128)}, f32[9,6,8,256]{3,2,1,0:T(8,128)}) custom-call(f32[9,6,1,2,8,256]{5,4,3,2,1,0:T(8,128)S(1)} %copy-done), custom_call_target="tpu_custom_call" | custom-call | tf_op jit(solution)/shard_map/split/pallas_call | solution.py:273
  2.8 3.0 %collective-permute-start.2 = (f32[9,6,8,256]{3,2,1,0:T(8,128)}, f32[9,6,8,256]{3,2,1,0:T(8,128)S(1)}, u32[]{:S(2)}, u32[]{:S(2)}) collective-permute-start(f32[9,6,8,256]{3,2,1,0:T(8,128)} %get-tuple-element.16), channel_id=1, source_target_pairs={{0,2},{2,0},{4,8},{6,10},{8,4},{10,6},{12,14},{14,12},{1,3},{3,1},... | collective-permute-start | bytes 1327112 | tf_op jit(solution)/shard_map/ppermute | solution.py:319
  5.8 1.7 %collective-permute-start.5 = (f32[9,6,8,256]{3,2,1,0:T(8,128)}, f32[9,6,8,256]{3,2,1,0:T(8,128)S(1)}, u32[]{:S(2)}, u32[]{:S(2)}) collective-permute-start(f32[9,6,8,256]{3,2,1,0:T(8,128)} %get-tuple-element.19), channel_id=1, source_target_pairs={{0,4},{2,6},{4,0},{6,2},{8,12},{10,14},{12,8},{14,10},{1,5},{3,7},... | collective-permute-start | bytes 1327112 | tf_op jit(solution)/shard_map/ppermute | solution.py:320
  7.5 0.0 copy-start.4
  7.5 0.0 copy-start.3
  7.5 0.2 faces.1
  7.7 0.0 copy-start.2
  7.7 0.0 copy-done.5
  7.7 0.4 %copy-done.4 = s32[2048]{0:T(1024)S(1)} copy-done((s32[2048]{0:T(1024)S(1)}, s32[2048]{0:T(1024)}, u32[]{:S(2)}) %copy-start.4) | copy-done | bytes 8216
  8.2 0.1 fusion.1
  8.3 0.0 copy-done.1
  8.3 3.6 %paired.1 = (f32[9,6,8,128]{3,2,1,0:T(8,128)S(1)}, f32[9,6,8,128]{3,2,1,0:T(8,128)S(1)}) custom-call(f32[9]{0:T(128)S(1)} %broadcast_select_fusion.turn, s32[8,256]{1,0:T(8,128)S(1)} %reshape.16.pairing, f32[9,6,1,2,8,256]{5,4,3,2,1,0:T(8,128)S(1)} %copy-done.1, f32[8,128]{1,0:T(8,128)S(1)} %get-tuple-element.15._), custom_call_target="tpu_custom_call" | custom-call | tf_op jit(solution)/shard_map/paired/pallas_call | solution.py:273
  11.9 1.7 %collective-permute-start.4 = (f32[9,6,8,128]{3,2,1,0:T(8,128)S(1)}, f32[9,6,8,128]{3,2,1,0:T(8,128)S(1)}, u32[]{:S(2)}, u32[]{:S(2)}) collective-permute-start(f32[9,6,8,128]{3,2,1,0:T(8,128)S(1)} %get-tuple-element.18), channel_id=1, source_target_pairs={{0,12},{2,14},{4,6},{6,4},{8,10},{10,8},{12,0},{14,2},{1,13},{3,15... | collective-permute-start | bytes 663560 | tf_op jit(solution)/shard_map/ppermute | solution.py:339
  13.7 2.2 %collective-permute-start.3 = (f32[9,6,8,128]{3,2,1,0:T(8,128)S(1)}, f32[9,6,8,128]{3,2,1,0:T(8,128)S(1)}, u32[]{:S(2)}, u32[]{:S(2)}) collective-permute-start(f32[9,6,8,128]{3,2,1,0:T(8,128)S(1)} %get-tuple-element.17), channel_id=1, source_target_pairs={{0,12},{2,14},{4,6},{6,4},{8,10},{10,8},{12,0},{14,2},{1,13},{3,15... | collective-permute-start | bytes 663560 | tf_op jit(solution)/shard_map/ppermute | solution.py:339
  15.8 0.0 collective-permute-start.1
  15.8 1.2 %collective-permute-done.1.span_ghost = f32[8,128]{1,0:T(8,128)S(1)} collective-permute-done((f32[8,128]{1,0:T(8,128)S(1)}, f32[8,128]{1,0:T(8,128)S(1)}, u32[]{:S(2)}, u32[]{:S(2)}) %collective-permute-start.1) | collective-permute-done | bytes 4128 | tf_op jit(solution)/shard_map/ppermute | solution.py:327
  17.0 1.5 %collective-permute-start = (f32[108,256]{1,0:T(8,128)S(1)}, f32[108,256]{1,0:T(8,128)S(1)}, u32[]{:S(2)}, u32[]{:S(2)}) collective-permute-start(f32[108,256]{1,0:T(8,128)S(1)} %get-tuple-element.14), channel_id=1, source_target_pairs={{0,2},{2,0},{4,6},{6,4},{8,10},{10,8},{12,14},{14,12},{1,3},{3,1},... | collective-permute-start | bytes 331784 | tf_op jit(solution)/shard_map/ppermute | solution.py:326
  18.5 3.7 %collective-permute-done.axial_ghost = f32[108,256]{1,0:T(8,128)S(1)} collective-permute-done((f32[108,256]{1,0:T(8,128)S(1)}, f32[108,256]{1,0:T(8,128)S(1)}, u32[]{:S(2)}, u32[]{:S(2)}) %collective-permute-start) | collective-permute-done | bytes 110624 | tf_op jit(solution)/shard_map/ppermute | solution.py:326
  22.2 0.0 copy-done.3
  22.2 0.0 copy-done.2
  22.2 1.8 %base.1.partial = f32[9,6,2,8,256]{4,3,2,1,0:T(8,128)S(1)} custom-call(f32[9,6,1,2,8,256]{5,4,3,2,1,0:T(8,128)S(1)} %copy-done.1, f32[9,6,1,2,8,256]{5,4,3,2,1,0:T(8,128)S(1)} %copy-done.3, f32[6,6,1,2,8,256]{5,4,3,2,1,0:T(8,128)S(1)} %copy-done.2, f32[108,256]{1,0:T(8,128)S(1)} %collective-permute-done.axial_ghost, ...), custom_call_target="tpu_custom_call" | custom-call | tf_op jit(solution)/shard_map/base/pallas_call | solution.py:273
  24.0 0.0 collective-permute-done.5.ghost
  24.0 2.0 %near.1 = (f32[9,6,1,2,8,256]{5,4,3,2,1,0:T(8,128)}, f32[9,6,1,2,8,256]{5,4,3,2,1,0:T(8,128)}) custom-call(f32[9,6,2,8,256]{4,3,2,1,0:T(8,128)S(1)} %base.1.partial, f32[9,6,1,2,8,256]{5,4,3,2,1,0:T(8,128)S(1)} %copy-done.1, f32[6,6,1,2,8,256]{5,4,3,2,1,0:T(8,128)S(1)} %copy-done.2, f32[9,6,8,256]{3,2,1,0:T(8,128)S(1)} %collective-permute-done.5.ghost), custom_call_target="tpu_custom_call" | custom-call | tf_op jit(solution)/shard_map/near/pallas_call | solution.py:273
  26.0 0.0 collective-permute-done.4.paired
  26.1 0.0 collective-permute-done.2.ghost
  26.1 1.3 %far.2 = (f32[9,6,1,2,8,256]{5,4,3,2,1,0:T(8,128)}, f32[9,6,1,2,8,256]{5,4,3,2,1,0:T(8,128)}) custom-call(f32[9,6,2,8,256]{4,3,2,1,0:T(8,128)S(1)} %base.1.partial, f32[9,6,1,2,8,256]{5,4,3,2,1,0:T(8,128)S(1)} %copy-done.1, f32[6,6,1,2,8,256]{5,4,3,2,1,0:T(8,128)S(1)} %copy-done.2, ...), custom_call_target="tpu_custom_call", output_to_operand_aliasing={{0}: (5, {}), {1}: (6, {})} | custom-call | tf_op jit(solution)/shard_map/far/pallas_call | solution.py:273
  27.4 1.6 %collective-permute-done.3.paired = f32[9,6,8,128]{3,2,1,0:T(8,128)S(1)} collective-permute-done((f32[9,6,8,128]{3,2,1,0:T(8,128)S(1)}, f32[9,6,8,128]{3,2,1,0:T(8,128)S(1)}, u32[]{:S(2)}, u32[]{:S(2)}) %collective-permute-start.3) | collective-permute-done | bytes 221216 | tf_op jit(solution)/shard_map/ppermute | solution.py:339
  29.0 1.3 %far.3 = (f32[9,6,1,2,8,256]{5,4,3,2,1,0:T(8,128)}, f32[9,6,1,2,8,256]{5,4,3,2,1,0:T(8,128)}) custom-call(f32[9,6,2,8,256]{4,3,2,1,0:T(8,128)S(1)} %base.1.partial, f32[9,6,1,2,8,256]{5,4,3,2,1,0:T(8,128)S(1)} %copy-done.1, f32[6,6,1,2,8,256]{5,4,3,2,1,0:T(8,128)S(1)} %copy-done.2, ...), custom_call_target="tpu_custom_call", output_to_operand_aliasing={{0}: (5, {}), {1}: (6, {})} | custom-call | tf_op jit(solution)/shard_map/far/pallas_call | solution.py:273
  (4 shorter events, 0.0 us)
Async XLA Ops:
  0.6 1.2 %copy-start = (f32[9,6,1,2,8,256]{5,4,3,2,1,0:T(8,128)S(1)}, f32[9,6,1,2,8,256]{5,4,3,2,1,0:T(8,128)}, u32[]{:S(2)}) copy-start(f32[9,6,1,2,8,256]{5,4,3,2,1,0:T(8,128)} %state.13) | copy-start | bytes 2654212
  1.8 5.9 %copy-start.5 = (s32[4]{0:T(128)S(1)}, s32[4]{0:T(128)}, u32[]{:S(2)}) copy-start(s32[4]{0:T(128)} %param.8) | copy-start | bytes 52
  1.8 6.5 %copy-start.1 = (f32[9,6,1,2,8,256]{5,4,3,2,1,0:T(8,128)S(1)}, f32[9,6,1,2,8,256]{5,4,3,2,1,0:T(8,128)}, u32[]{:S(2)}) copy-start(f32[9,6,1,2,8,256]{5,4,3,2,1,0:T(8,128)} %state.13) | copy-start | bytes 2654212
  2.8 23.3 %collective-permute-start.2 = (f32[9,6,8,256]{3,2,1,0:T(8,128)}, f32[9,6,8,256]{3,2,1,0:T(8,128)S(1)}, u32[]{:S(2)}, u32[]{:S(2)}) collective-permute-start(f32[9,6,8,256]{3,2,1,0:T(8,128)} %get-tuple-element.16), channel_id=1, source_target_pairs={{0,2},{2,0},{4,8},{6,10},{8,4},{10,6},{12,14},{14,12},{1,3},{3,1},... | collective-permute-start | bytes 1327112 | tf_op jit(solution)/shard_map/ppermute | solution.py:319
  5.8 18.2 %collective-permute-start.5 = (f32[9,6,8,256]{3,2,1,0:T(8,128)}, f32[9,6,8,256]{3,2,1,0:T(8,128)S(1)}, u32[]{:S(2)}, u32[]{:S(2)}) collective-permute-start(f32[9,6,8,256]{3,2,1,0:T(8,128)} %get-tuple-element.19), channel_id=1, source_target_pairs={{0,4},{2,6},{4,0},{6,2},{8,12},{10,14},{12,8},{14,10},{1,5},{3,7},... | collective-permute-start | bytes 1327112 | tf_op jit(solution)/shard_map/ppermute | solution.py:320
  7.5 0.7 %copy-start.4 = (s32[2048]{0:T(1024)S(1)}, s32[2048]{0:T(1024)}, u32[]{:S(2)}) copy-start(s32[2048]{0:T(1024)} %param.9) | copy-start | bytes 24580
  7.5 14.7 %copy-start.3 = (f32[9,6,1,2,8,256]{5,4,3,2,1,0:T(8,128)S(1)}, f32[9,6,1,2,8,256]{5,4,3,2,1,0:T(8,128)}, u32[]{:S(2)}) copy-start(f32[9,6,1,2,8,256]{5,4,3,2,1,0:T(8,128)} %source.1) | copy-start | bytes 2654212
  7.7 14.5 %copy-start.2 = (f32[6,6,1,2,8,256]{5,4,3,2,1,0:T(8,128)S(1)}, f32[6,6,1,2,8,256]{5,4,3,2,1,0:T(8,128)}, u32[]{:S(2)}) copy-start(f32[6,6,1,2,8,256]{5,4,3,2,1,0:T(8,128)} %matrix.7) | copy-start | bytes 1769476
  11.9 14.1 %collective-permute-start.4 = (f32[9,6,8,128]{3,2,1,0:T(8,128)S(1)}, f32[9,6,8,128]{3,2,1,0:T(8,128)S(1)}, u32[]{:S(2)}, u32[]{:S(2)}) collective-permute-start(f32[9,6,8,128]{3,2,1,0:T(8,128)S(1)} %get-tuple-element.18), channel_id=1, source_target_pairs={{0,12},{2,14},{4,6},{6,4},{8,10},{10,8},{12,0},{14,2},{1,13},{3,15... | collective-permute-start | bytes 663560 | tf_op jit(solution)/shard_map/ppermute | solution.py:339
  13.7 15.3 %collective-permute-start.3 = (f32[9,6,8,128]{3,2,1,0:T(8,128)S(1)}, f32[9,6,8,128]{3,2,1,0:T(8,128)S(1)}, u32[]{:S(2)}, u32[]{:S(2)}) collective-permute-start(f32[9,6,8,128]{3,2,1,0:T(8,128)S(1)} %get-tuple-element.17), channel_id=1, source_target_pairs={{0,12},{2,14},{4,6},{6,4},{8,10},{10,8},{12,0},{14,2},{1,13},{3,15... | collective-permute-start | bytes 663560 | tf_op jit(solution)/shard_map/ppermute | solution.py:339
  15.8 1.2 %collective-permute-start.1 = (f32[8,128]{1,0:T(8,128)S(1)}, f32[8,128]{1,0:T(8,128)S(1)}, u32[]{:S(2)}, u32[]{:S(2)}) collective-permute-start(f32[8,128]{1,0:T(8,128)S(1)} %get-tuple-element.15._), channel_id=1, source_target_pairs={{0,1},{1,0},{2,3},{3,2},{4,5},{5,4},{6,7},{7,6},{8,9},{9,8},{10,11... | collective-permute-start | bytes 12296 | tf_op jit(solution)/shard_map/ppermute | solution.py:327
  17.0 5.2 %collective-permute-start = (f32[108,256]{1,0:T(8,128)S(1)}, f32[108,256]{1,0:T(8,128)S(1)}, u32[]{:S(2)}, u32[]{:S(2)}) collective-permute-start(f32[108,256]{1,0:T(8,128)S(1)} %get-tuple-element.14), channel_id=1, source_target_pairs={{0,2},{2,0},{4,6},{6,4},{8,10},{10,8},{12,14},{14,12},{1,3},{3,1},... | collective-permute-start | bytes 331784 | tf_op jit(solution)/shard_map/ppermute | solution.py:326

commit v3 on v2

--- a/solution.py
+++ b/solution.py
@@ -83,16 +83,12 @@
     return near, 1 - near, ring == 0, ring == rings - 1, position % AXB, lax.axis_index("span")
 
 
-def split_kernel(state, far_face, near_face, sems):
-    near, far = places()[:2]
-    copies = [
-        pltpu.make_async_copy(state.at[:, :, 0, far], far_face, sems.at[0]),
-        pltpu.make_async_copy(state.at[:, :, 0, near], near_face, sems.at[1]),
-    ]
-    for copy in copies:
-        copy.start()
-    for copy in copies:
-        copy.wait()
+def layer_kernel(kind, state, *refs):
+    face = refs[-1]
+    c = places()[kind]
+    for i in range(state.shape[0]):
+        for v in range(state.shape[1]):
+            face[i, v] = state[i, v, 0, c]
 
 
 def paired_kernel(turn, pairing, state, _, *outs_and_scratch):
@@ -128,13 +124,14 @@
                             line = jnp.broadcast_to(line, (axial, LANES))
                             picked[i] = jnp.where(hit, take_lanes(line, lane), picked[i])
                 for n in range(instances):
-                    total = turn[n] * picked[0]
+                    total = turn[n : n + 1] * picked[0]
                     for m in range(1, instances):
-                        total = total + turn[(n - m) % instances] * picked[m]
+                        k = (n - m) % instances
+                        total = total + turn[k : k + 1] * picked[m]
                     out[n, v] = total
 
 
-def faces_kernel(state, axial_face, span_face):
+def faces_kernel(state, _, axial_face, span_face):
     instances, variables, _, circ, axial, span = state.shape
     _, _, _, _, axial_place, span_place = places()
     edge = jnp.where(axial_place == 0, axial - 1, 0)
@@ -173,14 +170,10 @@
     return update
 
 
-def base_kernel(state, source, matrix, axial_ghost, span_ghost, partial):
+def base_kernel(state, source, matrix, partial):
     instances, variables, _, circ, axial, span = state.shape
-    _, _, _, _, axial_place, span_place = places()
     row = lax.broadcasted_iota(jnp.int32, (axial, span), 0)
     column = lax.broadcasted_iota(jnp.int32, (axial, span), 1)
-    axial_row = jnp.where(axial_place == 0, axial - 1, 0)
-    span_column = jnp.where(span_place == 0, span - 1, 0)
-    columns = span_ghost[...]
 
     @pl.loop(0, circ * variables)
     def _(step):
@@ -189,38 +182,52 @@
         own = [state[i, v, 0, c] for i in range(instances)]
         timed = spectral_mix(own)
         for i in range(instances):
-            k = (c * instances + i) * variables + v
             near = state[i, v, 0, 1 - c]
             near = near + jnp.where(row == 0, 0.0, pltpu.roll(own[i], 1, 0))
             near = near + jnp.where(row == axial - 1, 0.0, pltpu.roll(own[i], axial - 1, 0))
-            near = near + jnp.where(row == axial_row, axial_ghost[pl.ds(k, 1), :], 0.0)
             near = near + jnp.where(column == 0, 0.0, pltpu.roll(own[i], 1, 1))
             near = near + jnp.where(column == span - 1, 0.0, pltpu.roll(own[i], span - 1, 1))
-            edge = take_lanes(columns, jnp.full((axial, LANES), k, jnp.int32))
-            edge = jnp.concatenate([edge] * (span // LANES), axis=1)
-            near = near + jnp.where(column == span_column, edge, 0.0)
             local = matrix[v, 0, 0, c] * state[i, 0, 0, c]
             for w in range(1, variables):
                 local = local + matrix[v, w, 0, c] * state[i, w, 0, c]
             partial[i, v, c] = source[i, v, 0, c] - (local - near + timed[i])
 
 
-def finish_tile(c, t, ghost, partial, state, matrix, residual, updated, buffers, sems):
-    instances, variables, _, axial, _ = partial.shape
+def edge_adder(shape, axial_ghost, span_ghost):
+    instances, variables, axial, span = shape
+    _, _, _, _, axial_place, span_place = places()
+    row = lax.broadcasted_iota(jnp.int32, (axial, span), 0)
+    column = lax.broadcasted_iota(jnp.int32, (axial, span), 1)
+    at_row = row == jnp.where(axial_place == 0, axial - 1, 0)
+    at_column = column == jnp.where(span_place == 0, span - 1, 0)
+    columns = span_ghost[...]
+
+    def add(value, c, i, v):
+        k = (c * instances + i) * variables + v
+        edge = take_lanes(columns, jnp.full((axial, LANES), k, jnp.int32))
+        edge = jnp.concatenate([edge] * (span // LANES), axis=1)
+        value = value + jnp.where(at_row, axial_ghost[pl.ds(k, 1), :], 0.0)
+        return value + jnp.where(at_column, edge, 0.0)
+
+    return add
+
+
+def finish_tile(c, t, right, state, matrix, residual, updated, buffers, sems):
+    instances, variables = state.shape[:2]
     lanes = slice(t * LANES, (t + 1) * LANES)
     copies = [
         pltpu.make_async_copy(buffers.at[n], whole.at[:, :, 0, c, :, lanes], sems.at[n])
         for n, whole in enumerate((residual, updated))
     ]
-    right = []
+    values = []
     for i in range(instances):
-        right.append([])
+        values.append([])
         for v in range(variables):
-            value = partial[i, v, c, :, lanes] + ghost(i, v, lanes)
+            value = right(i, v, lanes)
             buffers[0, i, v] = value
-            right[i].append(value)
+            values[i].append(value)
     copies[0].start()
-    update = solve_tile(right, lambda v, w: matrix[v, w, 0, c, :, lanes], (instances, variables))
+    update = solve_tile(values, lambda v, w: matrix[v, w, 0, c, :, lanes], (instances, variables))
     for i in range(instances):
         for v in range(variables):
             buffers[1, i, v] = state[i, v, 0, c, :, lanes] + update[i][v]
@@ -228,14 +235,36 @@
     return copies
 
 
-def near_kernel(partial, state, matrix, ghost, residual, updated, buffers, sems):
+def near_kernel(
+    partial,
+    state,
+    matrix,
+    near_ghost,
+    middle_ghost,
+    axial_ghost,
+    span_ghost,
+    residual,
+    updated,
+    waiting,
+    buffers,
+    sems,
+    total,
+):
+    near, far, first, last, _, _ = places()
+    shape = near_ghost.shape
+    add = edge_adder(shape, axial_ghost, span_ghost)
+
+    @pl.loop(0, shape[1])
+    def _(v):
+        for i in range(shape[0]):
+            total[i, v] = add(partial[i, v, near], near, i, v) + near_ghost[i, v]
+
     copies = []
-    for t in range(partial.shape[-1] // LANES):
+    for t in range(shape[-1] // LANES):
         copies += finish_tile(
-            places()[0],
+            near,
             t,
-            lambda i, v, lanes: ghost[i, v, :, lanes],
-            partial,
+            lambda i, v, lanes: total[i, v, :, lanes],
             state,
             matrix,
             residual,
@@ -243,17 +272,23 @@
             buffers.at[t],
             sems.at[t],
         )
+
+    @pl.loop(0, shape[1])
+    def _(v):
+        for i in range(shape[0]):
+            ghost = jnp.where(first | last, 0.0, middle_ghost[i, v])
+            waiting[i, v] = add(partial[i, v, far], far, i, v) + ghost
+
     for copy in copies:
         copy.wait()
 
 
-def far_kernel(t, partial, state, matrix, ghost, paired, _, __, residual, updated, buffers, sems):
+def far_kernel(t, waiting, state, matrix, paired, _, __, residual, updated, buffers, sems):
     _, far, first, last, _, _ = places()
     copies = finish_tile(
         far,
         t,
-        lambda i, v, lanes: jnp.where(first | last, paired[i, v], ghost[i, v, :, lanes]),
-        partial,
+        lambda i, v, lanes: waiting[i, v, :, lanes] + jnp.where(first | last, paired[i, v], 0.0),
         state,
         matrix,
         residual,
@@ -265,7 +300,7 @@
         copy.wait()
 
 
-def call(kernel, name, operands, outs, in_vmem=(), out_vmem=True, scratch=(), aliases=None):
+def call(kernel, name, operands, outs, ins, out_kinds=None, scratch=(), aliases=None):
     vmem = pl.BlockSpec(memory_space=pltpu.VMEM)
     anywhere = pl.BlockSpec(memory_space=pl.ANY)
     smem = pl.BlockSpec(memory_space=pltpu.SMEM)
@@ -273,8 +308,8 @@
     return pl.pallas_call(
         kernel,
         name=name,
-        in_specs=[kinds[k] for k in in_vmem],
-        out_specs=[vmem if out_vmem else anywhere] * len(outs),
+        in_specs=[kinds[k] for k in ins],
+        out_specs=[kinds[k] for k in out_kinds or "v" * len(outs)],
         out_shape=outs,
         scratch_shapes=scratch,
         input_output_aliases=aliases or {},
@@ -286,87 +321,98 @@
     instances, variables, _, circ, axial, span = state.shape
     tiles = span // LANES
     blocks = lax.axis_size("blocks")
+    cores = lax.axis_size("span")
     rings = blocks // AXB
 
     def array(*shape):
         return jax.ShapeDtypeStruct(shape, jnp.float32)
-
-    def across(block):
-        return block ^ 1
 
     def ring_partner(block, first):
         hop = 1 if block // AXB % 2 == first else -1
         return (block // AXB + hop) % rings * AXB + block % AXB
 
-    def at_end(block):
-        return block // AXB in (0, rings - 1)
-
-    every = range(blocks)
-    near_route = [(b, ring_partner(b, 0)) for b in every]
-    middle_route = [(b, across(b) if at_end(b) else ring_partner(b, 1)) for b in every]
-    paired_route = [(b, ring_partner(b, 1) if at_end(b) else across(b)) for b in every]
-    axial_route = [(b, across(b)) for b in every]
+    def far_route(ends):
+        route = []
+        for block in range(blocks):
+            for core in range(cores):
+                if (block // AXB in (0, rings - 1)) == ends:
+                    target = ring_partner(block, 1) * cores + core
+                else:
+                    target = block * cores + (core ^ 1)
+                route.append((block * cores + core, target))
+        return route
+
+    both = ("blocks", "span")
+    near_route = [(b, ring_partner(b, 0)) for b in range(blocks)]
+    axial_route = [(b, b ^ 1) for b in range(blocks)]
 
     layer = array(instances, variables, axial, span)
-    far_face, near_face = call(
-        split_kernel,
-        "split",
-        (state,),
-        [layer, layer],
-        "a",
-        scratch=[pltpu.SemaphoreType.DMA((2,))],
-    )
-    middle_ghost = lax.ppermute(far_face, "blocks", middle_route)
+    (far_face,) = call(
+        functools.partial(layer_kernel, 1), "far_layer", (state,), [layer], "v"
+    )
+    (near_face,) = call(
+        functools.partial(layer_kernel, 0), "near_layer", (state, far_face), [layer], "va"
+    )
+    middle_ghost = lax.ppermute(far_face, both, far_route(False))
     near_ghost = lax.ppermute(near_face, "blocks", near_route)
 
     faces = circ * instances * variables
     axial_face, span_face = call(
-        faces_kernel, "faces", (state,), [array(faces, span), array(axial, LANES)], "v"
+        faces_kernel,
+        "faces",
+        (state, near_face),
+        [array(faces, span), array(axial, LANES)],
+        "va",
     )
     axial_ghost = lax.ppermute(axial_face, "blocks", axial_route)
     span_ghost = lax.ppermute(span_face, "span", [(0, 1), (1, 0)])
 
     plus, minus = rotations(phase_index, instances)
     turn = jnp.where(lax.axis_index("blocks") < AXB, plus, minus)
+    turn = jnp.broadcast_to(turn[:, None], (instances, LANES))
+    chunks = [array(instances, variables, axial, LANES)] * tiles
     paired_faces = call(
         paired_kernel,
         "paired",
         (turn, face_pair.reshape(axial, span), state, span_face),
-        [array(instances, variables, axial, LANES)] * tiles,
-        "svva",
+        chunks,
+        "vvva",
         scratch=[pltpu.VMEM((tiles, axial, LANES), jnp.int32)],
     )
-    paired_ghosts = [lax.ppermute(face, "blocks", paired_route) for face in paired_faces]
+    paired_ghosts = [lax.ppermute(face, both, far_route(True)) for face in paired_faces]
 
     (partial,) = call(
         base_kernel,
         "base",
-        (state, source, block_matrix, axial_ghost, span_ghost),
+        (state, source, block_matrix),
         [array(instances, variables, circ, axial, span)],
-        "vvvvv",
-    )
-
+        "vvv",
+    )
     out = array(*state.shape)
     tile = (2, instances, variables, axial, LANES)
-    residual, updated = call(
+    residual, updated, waiting = call(
         near_kernel,
         "near",
-        (partial, state, block_matrix, near_ghost),
-        [out, out],
-        "vvvv",
-        out_vmem=False,
-        scratch=[pltpu.VMEM((tiles,) + tile, jnp.float32), pltpu.SemaphoreType.DMA((tiles, 2))],
+        (partial, state, block_matrix, near_ghost, middle_ghost, axial_ghost, span_ghost),
+        [out, out, layer],
+        "vvvvvvv",
+        "aav",
+        [
+            pltpu.VMEM((tiles,) + tile, jnp.float32),
+            pltpu.SemaphoreType.DMA((tiles, 2)),
+            pltpu.VMEM(layer.shape, jnp.float32),
+        ],
     )
     for t, ghost in enumerate(paired_ghosts):
         residual, updated = call(
             functools.partial(far_kernel, t),
             "far",
-            (partial, state, block_matrix, middle_ghost, ghost, residual, updated),
+            (waiting, state, block_matrix, ghost, residual, updated),
             [out, out],
-            "vvvvvaa",
-            out_vmem=False,
-            scratch=[pltpu.VMEM(tile, jnp.float32), pltpu.SemaphoreType.DMA((2,))],
-            aliases={5: 0, 6: 1},
+            "vvvvaa",
+            "aa",
+            [pltpu.VMEM(tile, jnp.float32), pltpu.SemaphoreType.DMA((2,))],
+            {4: 0, 5: 1},
         )
     return updated, residual
 

time: 30.5 us -> 28.9 us (0.948)
  waiting for transfers between devices: 6.48 us -> 4.94 us
    ppermute x1, starting transfers between devices: 1.66 us -> 4.21 us  [shards(): near_ghost = lax.ppermute(near_face, 'blocks', near_route)]
    ppermute x3, starting transfers between devices: 6.89 us -> 4.41 us  [the longest x2 3.89 us: shards(): lax.ppermute(face, both, far_route(True))]
    ppermute x1, waiting for transfers between devices: 3.73 us -> 2.27 us  [shards(): axial_ghost = lax.ppermute(axial_face, 'blocks', axial_route)]
    pallas_call x7 -> x8, Pallas kernels: 11.3 us -> 11 us  [call(): pl.pallas_call(kernel, name=name, in_specs=[kinds[k] for k in ins], out_s...]
  transfers between devices with their start and end apart: 6 -> 6, of which waited for: 3 -> 3; matrix products, arithmetic and copies ran while one was open for 1% -> 1% of each run, Pallas kernels for 30% -> 34%
where the time goes in v3:
time: 28.9 us; the launch traced here: 28.7 us
  Pallas kernels  11 us (38%)
  starting transfers between devices  10.1 us (35%)
  waiting for transfers between devices  4.94 us (17%)
  local copies, waits for them, and re-layouts  1.7 us (6%)
  between operations  0.73 us (3%)
    pallas_call x8, Pallas kernels, call(): pl.pallas_call(kernel, name=name, in_specs=[kinds[k] for k in ins], out_s...  11 us
    ppermute x1, starting transfers between devices, shards(): near_ghost = lax.ppermute(near_face, 'blocks', near_route)  4.21 us
    ppermute x2, starting transfers between devices, shards(): lax.ppermute(face, both, far_route(True))  3.89 us
    ppermute x1, waiting for transfers between devices, shards(): axial_ghost = lax.ppermute(axial_face, 'blocks', axial_route)  2.27 us
    unnamed x12, local copies, waits for them, and re-layouts  1.63 us
    ppermute x2, waiting for transfers between devices, shards(): lax.ppermute(face, both, far_route(True))  1.5 us
    ppermute x1, starting transfers between devices, shards(): axial_ghost = lax.ppermute(axial_face, 'blocks', axial_route)  1.49 us
    ppermute x1, waiting for transfers between devices, shards(): span_ghost = lax.ppermute(span_face, 'span', [(0, 1), (1, 0)])  1.16 us
  transfers between devices with their start and end apart: 6, of which 3 were waited for; matrix products, arithmetic and copies ran while one was open for 1% of the time, Pallas kernels for 34%

profile of v3, /device:TPU:0, one launch (start us, length us, event | category | flops | bytes accessed | tf_op | source)
XLA Modules:
  0.0 28.7 jit_solution(6286869146267845657)
XLA Ops:
  0.6 0.0 copy-start
  0.6 1.2 %copy-done = f32[9,6,1,2,8,256]{5,4,3,2,1,0:T(8,128)S(1)} copy-done((f32[9,6,1,2,8,256]{5,4,3,2,1,0:T(8,128)S(1)}, f32[9,6,1,2,8,256]{5,4,3,2,1,0:T(8,128)}, u32[]{:S(2)}) %copy-start) | copy-done | bytes 884760
  1.8 0.5 %collective-permute-start.1 = (f32[9,6,8,256]{3,2,1,0:T(8,128)S(1)}, f32[9,6,8,256]{3,2,1,0:T(8,128)}, u32[]{:S(2)}, u32[]{:S(2)}) collective-permute-start(f32[9,6,8,256]{3,2,1,0:T(8,128)S(1)} %far_layer.1.refs_0_), channel_id=1, source_target_pairs={{0,1},{1,0},{2,3},{3,2},{4,8},{5,9},{6,10},{7,11},{8,4},{9,5},{10,... | collective-permute-start | bytes 1327112 | tf_op jit(solution)/shard_map/ppermute | solution.py:356
  2.4 0.0 copy-start.3
  2.4 0.0 copy-start.1
  2.4 4.2 %collective-permute-start = (f32[9,6,8,256]{3,2,1,0:T(8,128)S(1)}, f32[9,6,8,256]{3,2,1,0:T(8,128)}, u32[]{:S(2)}, u32[]{:S(2)}) collective-permute-start(f32[9,6,8,256]{3,2,1,0:T(8,128)S(1)} %near_layer.1._), channel_id=1, source_target_pairs={{0,4},{2,6},{4,0},{6,2},{8,12},{10,14},{12,8},{14,10},{1,5},{3,7},... | collective-permute-start | bytes 1327112 | tf_op jit(solution)/shard_map/ppermute | solution.py:357
  6.6 0.0 copy-start.5
  6.6 0.0 copy-start.4
  6.6 0.2 faces.1
  6.8 0.0 copy-start.2
  6.9 0.4 %copy-done.5 = s32[4]{0:T(128)S(1)} copy-done((s32[4]{0:T(128)S(1)}, s32[4]{0:T(128)}, u32[]{:S(2)}) %copy-start.5) | copy-done | bytes 40
  7.3 0.0 copy-done.4
  7.3 0.1 fusion.1
  7.5 0.1 broadcast_in_dim.2.turn
  7.5 0.0 copy-done.1
  7.5 3.1 %paired.1 = (f32[9,6,8,128]{3,2,1,0:T(8,128)S(1)}, f32[9,6,8,128]{3,2,1,0:T(8,128)S(1)}) custom-call(f32[9,128]{1,0:T(8,128)S(1)} %broadcast_in_dim.2.turn, s32[8,256]{1,0:T(8,128)S(1)} %reshape.27.pairing, f32[9,6,1,2,8,256]{5,4,3,2,1,0:T(8,128)S(1)} %copy-done.1, f32[8,128]{1,0:T(8,128)S(1)} %get-tuple-element.14._), custom_call_target="tpu_custom_call" | custom-call | tf_op jit(solution)/shard_map/paired/pallas_call | solution.py:308
  10.6 1.1 %collective-permute-start.5 = (f32[9,6,8,128]{3,2,1,0:T(8,128)S(1)}, f32[9,6,8,128]{3,2,1,0:T(8,128)S(1)}, u32[]{:S(2)}, u32[]{:S(2)}) collective-permute-start(f32[9,6,8,128]{3,2,1,0:T(8,128)S(1)} %get-tuple-element.17), channel_id=1, source_target_pairs={{0,12},{1,13},{2,14},{3,15},{4,5},{5,4},{6,7},{7,6},{8,9},{9,8},{1... | collective-permute-start | bytes 663560 | tf_op jit(solution)/shard_map/ppermute | solution.py:382
  11.7 2.8 %collective-permute-start.4 = (f32[9,6,8,128]{3,2,1,0:T(8,128)S(1)}, f32[9,6,8,128]{3,2,1,0:T(8,128)S(1)}, u32[]{:S(2)}, u32[]{:S(2)}) collective-permute-start(f32[9,6,8,128]{3,2,1,0:T(8,128)S(1)} %get-tuple-element.16), channel_id=1, source_target_pairs={{0,12},{1,13},{2,14},{3,15},{4,5},{5,4},{6,7},{7,6},{8,9},{9,8},{1... | collective-permute-start | bytes 663560 | tf_op jit(solution)/shard_map/ppermute | solution.py:382
  14.5 0.0 collective-permute-start.3
  14.5 1.2 %collective-permute-done.3.span_ghost = f32[8,128]{1,0:T(8,128)S(1)} collective-permute-done((f32[8,128]{1,0:T(8,128)S(1)}, f32[8,128]{1,0:T(8,128)S(1)}, u32[]{:S(2)}, u32[]{:S(2)}) %collective-permute-start.3) | collective-permute-done | bytes 4128 | tf_op jit(solution)/shard_map/ppermute | solution.py:368
  15.7 1.5 %collective-permute-start.2 = (f32[108,256]{1,0:T(8,128)S(1)}, f32[108,256]{1,0:T(8,128)S(1)}, u32[]{:S(2)}, u32[]{:S(2)}) collective-permute-start(f32[108,256]{1,0:T(8,128)S(1)} %get-tuple-element.13), channel_id=1, source_target_pairs={{0,2},{2,0},{4,6},{6,4},{8,10},{10,8},{12,14},{14,12},{1,3},{3,1},... | collective-permute-start | bytes 331784 | tf_op jit(solution)/shard_map/ppermute | solution.py:367
  17.2 0.0 copy-done.3
  17.2 0.0 copy-done.2
  17.2 1.4 %base.1.partial = f32[9,6,2,8,256]{4,3,2,1,0:T(8,128)S(1)} custom-call(f32[9,6,1,2,8,256]{5,4,3,2,1,0:T(8,128)S(1)} %copy-done.1, f32[9,6,1,2,8,256]{5,4,3,2,1,0:T(8,128)S(1)} %copy-done.3, f32[6,6,1,2,8,256]{5,4,3,2,1,0:T(8,128)S(1)} %copy-done.2), custom_call_target="tpu_custom_call" | custom-call | tf_op jit(solution)/shard_map/base/pallas_call | solution.py:308
  18.6 2.3 %collective-permute-done.2.axial_ghost = f32[108,256]{1,0:T(8,128)S(1)} collective-permute-done((f32[108,256]{1,0:T(8,128)S(1)}, f32[108,256]{1,0:T(8,128)S(1)}, u32[]{:S(2)}, u32[]{:S(2)}) %collective-permute-start.2) | collective-permute-done | bytes 110624 | tf_op jit(solution)/shard_map/ppermute | solution.py:367
  20.9 0.0 collective-permute-done.near_ghost
  20.9 0.0 collective-permute-done.1.middle_ghost
  20.9 3.7 %near.1 = (f32[9,6,1,2,8,256]{5,4,3,2,1,0:T(8,128)}, f32[9,6,1,2,8,256]{5,4,3,2,1,0:T(8,128)}, f32[9,6,8,256]{3,2,1,0:T(8,128)S(1)}) custom-call(f32[9,6,2,8,256]{4,3,2,1,0:T(8,128)S(1)} %base.1.partial, f32[9,6,1,2,8,256]{5,4,3,2,1,0:T(8,128)S(1)} %copy-done.1, f32[6,6,1,2,8,256]{5,4,3,2,1,0:T(8,128)S(1)} %copy-done.2, ...), custom_call_target="tpu_custom_call" | custom-call | tf_op jit(solution)/shard_map/near/pallas_call | solution.py:308
  24.6 0.0 collective-permute-done.5.paired
  24.6 1.3 %far.2 = (f32[9,6,1,2,8,256]{5,4,3,2,1,0:T(8,128)}, f32[9,6,1,2,8,256]{5,4,3,2,1,0:T(8,128)}) custom-call(f32[9,6,8,256]{3,2,1,0:T(8,128)S(1)} %get-tuple-element.15.waiting, f32[9,6,1,2,8,256]{5,4,3,2,1,0:T(8,128)S(1)} %copy-done.1, f32[6,6,1,2,8,256]{5,4,3,2,1,0:T(8,128)S(1)} %copy-done.2, ...), custom_call_target="tpu_custom_call", output_to_operand_aliasing={{0}: (4, {}), {1}: (5, {})} | custom-call | tf_op jit(solution)/shard_map/far/pallas_call | solution.py:308
  25.9 1.5 %collective-permute-done.4.paired = f32[9,6,8,128]{3,2,1,0:T(8,128)S(1)} collective-permute-done((f32[9,6,8,128]{3,2,1,0:T(8,128)S(1)}, f32[9,6,8,128]{3,2,1,0:T(8,128)S(1)}, u32[]{:S(2)}, u32[]{:S(2)}) %collective-permute-start.4) | collective-permute-done | bytes 221216 | tf_op jit(solution)/shard_map/ppermute | solution.py:382
  27.4 1.3 %far.3 = (f32[9,6,1,2,8,256]{5,4,3,2,1,0:T(8,128)}, f32[9,6,1,2,8,256]{5,4,3,2,1,0:T(8,128)}) custom-call(f32[9,6,8,256]{3,2,1,0:T(8,128)S(1)} %get-tuple-element.15.waiting, f32[9,6,1,2,8,256]{5,4,3,2,1,0:T(8,128)S(1)} %copy-done.1, f32[6,6,1,2,8,256]{5,4,3,2,1,0:T(8,128)S(1)} %copy-done.2, ...), custom_call_target="tpu_custom_call", output_to_operand_aliasing={{0}: (4, {}), {1}: (5, {})} | custom-call | tf_op jit(solution)/shard_map/far/pallas_call | solution.py:308
  (6 shorter events, 0.1 us)
Async XLA Ops:
  0.6 1.2 %copy-start = (f32[9,6,1,2,8,256]{5,4,3,2,1,0:T(8,128)S(1)}, f32[9,6,1,2,8,256]{5,4,3,2,1,0:T(8,128)}, u32[]{:S(2)}) copy-start(f32[9,6,1,2,8,256]{5,4,3,2,1,0:T(8,128)} %state.15) | copy-start | bytes 2654212
  1.8 19.1 %collective-permute-start.1 = (f32[9,6,8,256]{3,2,1,0:T(8,128)S(1)}, f32[9,6,8,256]{3,2,1,0:T(8,128)}, u32[]{:S(2)}, u32[]{:S(2)}) collective-permute-start(f32[9,6,8,256]{3,2,1,0:T(8,128)S(1)} %far_layer.1.refs_0_), channel_id=1, source_target_pairs={{0,1},{1,0},{2,3},{3,2},{4,8},{5,9},{6,10},{7,11},{8,4},{9,5},{10,... | collective-permute-start | bytes 1327112 | tf_op jit(solution)/shard_map/ppermute | solution.py:356
  2.4 14.8 %copy-start.3 = (f32[9,6,1,2,8,256]{5,4,3,2,1,0:T(8,128)S(1)}, f32[9,6,1,2,8,256]{5,4,3,2,1,0:T(8,128)}, u32[]{:S(2)}) copy-start(f32[9,6,1,2,8,256]{5,4,3,2,1,0:T(8,128)} %source.1) | copy-start | bytes 2654212
  2.4 5.2 %copy-start.1 = (f32[9,6,1,2,8,256]{5,4,3,2,1,0:T(8,128)S(1)}, f32[9,6,1,2,8,256]{5,4,3,2,1,0:T(8,128)}, u32[]{:S(2)}) copy-start(f32[9,6,1,2,8,256]{5,4,3,2,1,0:T(8,128)} %state.15) | copy-start | bytes 2654212
  2.4 18.5 %collective-permute-start = (f32[9,6,8,256]{3,2,1,0:T(8,128)S(1)}, f32[9,6,8,256]{3,2,1,0:T(8,128)}, u32[]{:S(2)}, u32[]{:S(2)}) collective-permute-start(f32[9,6,8,256]{3,2,1,0:T(8,128)S(1)} %near_layer.1._), channel_id=1, source_target_pairs={{0,4},{2,6},{4,0},{6,2},{8,12},{10,14},{12,8},{14,10},{1,5},{3,7},... | collective-permute-start | bytes 1327112 | tf_op jit(solution)/shard_map/ppermute | solution.py:357
  6.6 0.7 %copy-start.5 = (s32[4]{0:T(128)S(1)}, s32[4]{0:T(128)}, u32[]{:S(2)}) copy-start(s32[4]{0:T(128)} %param.8) | copy-start | bytes 52
  6.6 0.7 %copy-start.4 = (s32[2048]{0:T(1024)S(1)}, s32[2048]{0:T(1024)}, u32[]{:S(2)}) copy-start(s32[2048]{0:T(1024)} %param.9) | copy-start | bytes 24580
  6.8 10.3 %copy-start.2 = (f32[6,6,1,2,8,256]{5,4,3,2,1,0:T(8,128)S(1)}, f32[6,6,1,2,8,256]{5,4,3,2,1,0:T(8,128)}, u32[]{:S(2)}) copy-start(f32[6,6,1,2,8,256]{5,4,3,2,1,0:T(8,128)} %matrix.7) | copy-start | bytes 1769476
  10.6 13.9 %collective-permute-start.5 = (f32[9,6,8,128]{3,2,1,0:T(8,128)S(1)}, f32[9,6,8,128]{3,2,1,0:T(8,128)S(1)}, u32[]{:S(2)}, u32[]{:S(2)}) collective-permute-start(f32[9,6,8,128]{3,2,1,0:T(8,128)S(1)} %get-tuple-element.17), channel_id=1, source_target_pairs={{0,12},{1,13},{2,14},{3,15},{4,5},{5,4},{6,7},{7,6},{8,9},{9,8},{1... | collective-permute-start | bytes 663560 | tf_op jit(solution)/shard_map/ppermute | solution.py:382
  11.7 15.7 %collective-permute-start.4 = (f32[9,6,8,128]{3,2,1,0:T(8,128)S(1)}, f32[9,6,8,128]{3,2,1,0:T(8,128)S(1)}, u32[]{:S(2)}, u32[]{:S(2)}) collective-permute-start(f32[9,6,8,128]{3,2,1,0:T(8,128)S(1)} %get-tuple-element.16), channel_id=1, source_target_pairs={{0,12},{1,13},{2,14},{3,15},{4,5},{5,4},{6,7},{7,6},{8,9},{9,8},{1... | collective-permute-start | bytes 663560 | tf_op jit(solution)/shard_map/ppermute | solution.py:382
  14.5 1.2 %collective-permute-start.3 = (f32[8,128]{1,0:T(8,128)S(1)}, f32[8,128]{1,0:T(8,128)S(1)}, u32[]{:S(2)}, u32[]{:S(2)}) collective-permute-start(f32[8,128]{1,0:T(8,128)S(1)} %get-tuple-element.14._), channel_id=1, source_target_pairs={{0,1},{1,0},{2,3},{3,2},{4,5},{5,4},{6,7},{7,6},{8,9},{9,8},{10,11... | collective-permute-start | bytes 12296 | tf_op jit(solution)/shard_map/ppermute | solution.py:368
  15.7 5.2 %collective-permute-start.2 = (f32[108,256]{1,0:T(8,128)S(1)}, f32[108,256]{1,0:T(8,128)S(1)}, u32[]{:S(2)}, u32[]{:S(2)}) collective-permute-start(f32[108,256]{1,0:T(8,128)S(1)} %get-tuple-element.13), channel_id=1, source_target_pairs={{0,2},{2,0},{4,6},{6,4},{8,10},{10,8},{12,14},{14,12},{1,3},{3,1},... | collective-permute-start | bytes 331784 | tf_op jit(solution)/shard_map/ppermute | solution.py:367

commit v4 on v3

--- a/solution.py
+++ b/solution.py
@@ -150,30 +150,86 @@
     span_face[...] = columns
 
 
+def harmonic_tables(instances):
+    harmonics = range(1, (instances - 1) // 2 + 1)
+    turn = 2.0 * math.pi / instances
+    cosines = [[math.cos(turn * k * n) for n in harmonics] for k in harmonics]
+    sines = [[math.sin(turn * k * n) for n in harmonics] for k in harmonics]
+    return cosines, sines
+
+
+def weighted(weights, values):
+    total = weights[0] * values[0]
+    for weight, value in zip(weights[1:], values[1:]):
+        total = total + weight * value
+    return total
+
+
+def to_harmonics(values):
+    count = len(values)
+    half = range(1, (count - 1) // 2 + 1)
+    cosines, sines = harmonic_tables(count)
+    even = [values[n] + values[count - n] for n in half]
+    odd = [values[n] - values[count - n] for n in half]
+    modes = [sum(even[1:], values[0] + even[0])]
+    for k in range(len(half)):
+        modes.append(values[0] + weighted(cosines[k], even))
+        modes.append(weighted(sines[k], odd))
+    return modes
+
+
+def from_harmonics(modes):
+    count = len(modes)
+    harmonics = range((count - 1) // 2)
+    cosines, sines = harmonic_tables(count)
+    mean = modes[0] * (1.0 / count)
+    cosine = [modes[2 * k + 1] * (2.0 / count) for k in harmonics]
+    sine = [modes[2 * k + 2] * (2.0 / count) for k in harmonics]
+    values = [None] * count
+    values[0] = sum(cosine[1:], mean + cosine[0])
+    for n in harmonics:
+        even = mean + weighted([cosines[k][n] for k in harmonics], cosine)
+        odd = weighted([sines[k][n] for k in harmonics], sine)
+        values[n + 1] = even + odd
+        values[count - n - 1] = even - odd
+    return values
+
+
 def solve_tile(residual, matrix, count):
     instances, variables = count
     scale = [1.0 / matrix(v, v) for v in range(variables)]
-    first = [[residual[i][v] * scale[v] for v in range(variables)] for i in range(instances)]
+    first = [
+        [mode * scale[v] for mode in to_harmonics([residual[i][v] for i in range(instances)])]
+        for v in range(variables)
+    ]
     update = first
     for _ in range(NSWEEP):
-        later = [[None] * variables for _ in range(instances)]
+        later = []
         for v in range(variables):
-            total = spectral_mix([update[i][v] for i in range(instances)])
+            total = [None] * instances
+            for k in range(1, (instances - 1) // 2 + 1):
+                total[2 * k - 1] = float(k) * update[v][2 * k]
+                total[2 * k] = -float(k) * update[v][2 * k - 1]
             for w in range(variables):
                 if w != v:
                     entry = matrix(v, w)
-                    for i in range(instances):
-                        total[i] = total[i] + entry * update[i][w]
-            for i in range(instances):
-                later[i][v] = first[i][v] - scale[v] * total[i]
+                    for m in range(instances):
+                        term = entry * update[w][m]
+                        total[m] = term if total[m] is None else total[m] + term
+            later.append([first[v][m] - scale[v] * total[m] for m in range(instances)])
         update = later
-    return update
-
-
-def base_kernel(state, source, matrix, partial):
+    solved = [from_harmonics(modes) for modes in update]
+    return [[solved[v][i] for v in range(variables)] for i in range(instances)]
+
+
+def base_kernel(state, source, matrix, axial_ghost, span_ghost, partial):
     instances, variables, _, circ, axial, span = state.shape
+    _, _, _, _, axial_place, span_place = places()
     row = lax.broadcasted_iota(jnp.int32, (axial, span), 0)
     column = lax.broadcasted_iota(jnp.int32, (axial, span), 1)
+    axial_row = jnp.where(axial_place == 0, axial - 1, 0)
+    span_column = jnp.where(span_place == 0, span - 1, 0)
+    columns = span_ghost[...]
 
     @pl.loop(0, circ * variables)
     def _(step):
@@ -182,34 +238,20 @@
         own = [state[i, v, 0, c] for i in range(instances)]
         timed = spectral_mix(own)
         for i in range(instances):
+            k = (c * instances + i) * variables + v
             near = state[i, v, 0, 1 - c]
             near = near + jnp.where(row == 0, 0.0, pltpu.roll(own[i], 1, 0))
             near = near + jnp.where(row == axial - 1, 0.0, pltpu.roll(own[i], axial - 1, 0))
+            near = near + jnp.where(row == axial_row, axial_ghost[pl.ds(k, 1), :], 0.0)
             near = near + jnp.where(column == 0, 0.0, pltpu.roll(own[i], 1, 1))
             near = near + jnp.where(column == span - 1, 0.0, pltpu.roll(own[i], span - 1, 1))
+            edge = take_lanes(columns, jnp.full((axial, LANES), k, jnp.int32))
+            edge = jnp.concatenate([edge] * (span // LANES), axis=1)
+            near = near + jnp.where(column == span_column, edge, 0.0)
             local = matrix[v, 0, 0, c] * state[i, 0, 0, c]
             for w in range(1, variables):
                 local = local + matrix[v, w, 0, c] * state[i, w, 0, c]
             partial[i, v, c] = source[i, v, 0, c] - (local - near + timed[i])
-
-
-def edge_adder(shape, axial_ghost, span_ghost):
-    instances, variables, axial, span = shape
-    _, _, _, _, axial_place, span_place = places()
-    row = lax.broadcasted_iota(jnp.int32, (axial, span), 0)
-    column = lax.broadcasted_iota(jnp.int32, (axial, span), 1)
-    at_row = row == jnp.where(axial_place == 0, axial - 1, 0)
-    at_column = column == jnp.where(span_place == 0, span - 1, 0)
-    columns = span_ghost[...]
-
-    def add(value, c, i, v):
-        k = (c * instances + i) * variables + v
-        edge = take_lanes(columns, jnp.full((axial, LANES), k, jnp.int32))
-        edge = jnp.concatenate([edge] * (span // LANES), axis=1)
-        value = value + jnp.where(at_row, axial_ghost[pl.ds(k, 1), :], 0.0)
-        return value + jnp.where(at_column, edge, 0.0)
-
-    return add
 
 
 def finish_tile(c, t, right, state, matrix, residual, updated, buffers, sems):
@@ -235,36 +277,14 @@
     return copies
 
 
-def near_kernel(
-    partial,
-    state,
-    matrix,
-    near_ghost,
-    middle_ghost,
-    axial_ghost,
-    span_ghost,
-    residual,
-    updated,
-    waiting,
-    buffers,
-    sems,
-    total,
-):
-    near, far, first, last, _, _ = places()
-    shape = near_ghost.shape
-    add = edge_adder(shape, axial_ghost, span_ghost)
-
-    @pl.loop(0, shape[1])
-    def _(v):
-        for i in range(shape[0]):
-            total[i, v] = add(partial[i, v, near], near, i, v) + near_ghost[i, v]
-
+def near_kernel(partial, state, matrix, ghost, residual, updated, buffers, sems):
+    near = places()[0]
     copies = []
-    for t in range(shape[-1] // LANES):
+    for t in range(partial.shape[-1] // LANES):
         copies += finish_tile(
             near,
             t,
-            lambda i, v, lanes: total[i, v, :, lanes],
+            lambda i, v, lanes: partial[i, v, near, :, lanes] + ghost[i, v, :, lanes],
             state,
             matrix,
             residual,
@@ -272,30 +292,18 @@
             buffers.at[t],
             sems.at[t],
         )
-
-    @pl.loop(0, shape[1])
-    def _(v):
-        for i in range(shape[0]):
-            ghost = jnp.where(first | last, 0.0, middle_ghost[i, v])
-            waiting[i, v] = add(partial[i, v, far], far, i, v) + ghost
-
     for copy in copies:
         copy.wait()
 
 
-def far_kernel(t, waiting, state, matrix, paired, _, __, residual, updated, buffers, sems):
+def far_kernel(t, partial, state, matrix, middle, paired, _, __, residual, updated, buffers, sems):
     _, far, first, last, _, _ = places()
-    copies = finish_tile(
-        far,
-        t,
-        lambda i, v, lanes: waiting[i, v, :, lanes] + jnp.where(first | last, paired[i, v], 0.0),
-        state,
-        matrix,
-        residual,
-        updated,
-        buffers,
-        sems,
-    )
+
+    def right(i, v, lanes):
+        ghost = jnp.where(first | last, paired[i, v], middle[i, v, :, lanes])
+        return partial[i, v, far, :, lanes] + ghost
+
+    copies = finish_tile(far, t, right, state, matrix, residual, updated, buffers, sems)
     for copy in copies:
         copy.wait()
 
@@ -347,20 +355,20 @@
     axial_route = [(b, b ^ 1) for b in range(blocks)]
 
     layer = array(instances, variables, axial, span)
+    (near_face,) = call(
+        functools.partial(layer_kernel, 0), "near_layer", (state,), [layer], "v"
+    )
+    near_ghost = lax.ppermute(near_face, "blocks", near_route)
     (far_face,) = call(
-        functools.partial(layer_kernel, 1), "far_layer", (state,), [layer], "v"
-    )
-    (near_face,) = call(
-        functools.partial(layer_kernel, 0), "near_layer", (state, far_face), [layer], "va"
+        functools.partial(layer_kernel, 1), "far_layer", (state, near_face), [layer], "va"
     )
     middle_ghost = lax.ppermute(far_face, both, far_route(False))
-    near_ghost = lax.ppermute(near_face, "blocks", near_route)
 
     faces = circ * instances * variables
     axial_face, span_face = call(
         faces_kernel,
         "faces",
-        (state, near_face),
+        (state, far_face),
         [array(faces, span), array(axial, LANES)],
         "va",
     )
@@ -384,35 +392,31 @@
     (partial,) = call(
         base_kernel,
         "base",
-        (state, source, block_matrix),
+        (state, source, block_matrix, axial_ghost, span_ghost),
         [array(instances, variables, circ, axial, span)],
-        "vvv",
+        "vvvvv",
     )
     out = array(*state.shape)
     tile = (2, instances, variables, axial, LANES)
-    residual, updated, waiting = call(
+    residual, updated = call(
         near_kernel,
         "near",
-        (partial, state, block_matrix, near_ghost, middle_ghost, axial_ghost, span_ghost),
-        [out, out, layer],
-        "vvvvvvv",
-        "aav",
-        [
-            pltpu.VMEM((tiles,) + tile, jnp.float32),
-            pltpu.SemaphoreType.DMA((tiles, 2)),
-            pltpu.VMEM(layer.shape, jnp.float32),
-        ],
+        (partial, state, block_matrix, near_ghost),
+        [out, out],
+        "vvvv",
+        "aa",
+        [pltpu.VMEM((tiles,) + tile, jnp.float32), pltpu.SemaphoreType.DMA((tiles, 2))],
     )
     for t, ghost in enumerate(paired_ghosts):
         residual, updated = call(
             functools.partial(far_kernel, t),
             "far",
-            (waiting, state, block_matrix, ghost, residual, updated),
+            (partial, state, block_matrix, middle_ghost, ghost, residual, updated),
             [out, out],
-            "vvvvaa",
+            "vvvvvaa",
             "aa",
             [pltpu.VMEM(tile, jnp.float32), pltpu.SemaphoreType.DMA((2,))],
-            {4: 0, 5: 1},
+            {5: 0, 6: 1},
         )
     return updated, residual
 

time: 28.9 us -> 28.3 us (0.979)
  Pallas kernels: 11 us -> 9.17 us
  starting transfers between devices: 10.1 us -> 8.54 us
  waiting for transfers between devices: 4.94 us -> 6.39 us
  local copies, waits for them, and re-layouts: 1.7 us -> 3.02 us
    pallas_call x8, Pallas kernels: 11 us -> 9.17 us  [call(): pl.pallas_call(kernel, name=name, in_specs=[kinds[k] for k in ins], out_s...]
    ppermute x1, waiting for transfers between devices: 2.27 us -> 3.73 us  [shards(): axial_ghost = lax.ppermute(axial_face, 'blocks', axial_route)]
    unnamed x12, local copies, waits for them, and re-layouts: 1.63 us -> 2.94 us
    ppermute x1, starting transfers between devices: 4.21 us -> 3.09 us  [shards(): near_ghost = lax.ppermute(near_face, 'blocks', near_route)]
    ppermute x1, starting transfers between devices: 0.52 us -> 0.07 us  [shards(): middle_ghost = lax.ppermute(far_face, both, far_route(False))]
  transfers between devices with their start and end apart: 6 -> 6, of which waited for: 3 -> 3; matrix products, arithmetic and copies ran while one was open for 1% -> 1% of each run, Pallas kernels for 34% -> 28%
where the time goes in v4:
time: 28.3 us; the launch traced here: 28 us
  Pallas kernels  9.17 us (32%)
  starting transfers between devices  8.54 us (30%)
  waiting for transfers between devices  6.39 us (23%)
  local copies, waits for them, and re-layouts  3.02 us (11%)
  between operations  0.77 us (3%)
    pallas_call x8, Pallas kernels, call(): pl.pallas_call(kernel, name=name, in_specs=[kinds[k] for k in ins], out_s...  9.17 us
    ppermute x2, starting transfers between devices, shards(): lax.ppermute(face, both, far_route(True))  3.89 us
    ppermute x1, waiting for transfers between devices, shards(): axial_ghost = lax.ppermute(axial_face, 'blocks', axial_route)  3.73 us
    ppermute x1, starting transfers between devices, shards(): near_ghost = lax.ppermute(near_face, 'blocks', near_route)  3.09 us
    unnamed x12, local copies, waits for them, and re-layouts  2.94 us
    ppermute x2, waiting for transfers between devices, shards(): lax.ppermute(face, both, far_route(True))  1.49 us
    ppermute x1, starting transfers between devices, shards(): axial_ghost = lax.ppermute(axial_face, 'blocks', axial_route)  1.49 us
    ppermute x1, waiting for transfers between devices, shards(): span_ghost = lax.ppermute(span_face, 'span', [(0, 1), (1, 0)])  1.16 us
  transfers between devices with their start and end apart: 6, of which 3 were waited for; matrix products, arithmetic and copies ran while one was open for 1% of the time, Pallas kernels for 28%

profile of v4, /device:TPU:0, one launch (start us, length us, event | category | flops | bytes accessed | tf_op | source)
XLA Modules:
  0.0 28.0 jit_solution(4374752299977095917)
XLA Ops:
  0.6 0.0 copy-start
  0.6 1.2 %copy-done = f32[9,6,1,2,8,256]{5,4,3,2,1,0:T(8,128)S(1)} copy-done((f32[9,6,1,2,8,256]{5,4,3,2,1,0:T(8,128)S(1)}, f32[9,6,1,2,8,256]{5,4,3,2,1,0:T(8,128)}, u32[]{:S(2)}) %copy-start) | copy-done | bytes 884760
  1.8 3.1 %collective-permute-start.5 = (f32[9,6,8,256]{3,2,1,0:T(8,128)S(1)}, f32[9,6,8,256]{3,2,1,0:T(8,128)S(1)}, u32[]{:S(2)}, u32[]{:S(2)}) collective-permute-start(f32[9,6,8,256]{3,2,1,0:T(8,128)S(1)} %near_layer.1.refs_0_), channel_id=1, source_target_pairs={{0,4},{2,6},{4,0},{6,2},{8,12},{10,14},{12,8},{14,10},{1,5},{3,7},... | collective-permute-start | bytes 1327112 | tf_op jit(solution)/shard_map/ppermute | solution.py:361
  5.0 0.0 copy-start.1
  5.0 0.1 collective-permute-start.2
  5.1 0.0 copy-start.5
  5.1 0.0 copy-start.4
  5.1 0.2 faces.1
  5.3 0.0 copy-start.2
  5.3 0.4 %copy-done.5 = s32[4]{0:T(128)S(1)} copy-done((s32[4]{0:T(128)S(1)}, s32[4]{0:T(128)}, u32[]{:S(2)}) %copy-start.5) | copy-done | bytes 40
  5.8 0.0 copy-done.4
  5.8 0.1 fusion.1
  6.0 0.1 broadcast_in_dim.2.turn
  6.1 0.1 copy-done.1
  6.2 3.1 %paired.1 = (f32[9,6,8,128]{3,2,1,0:T(8,128)S(1)}, f32[9,6,8,128]{3,2,1,0:T(8,128)S(1)}) custom-call(f32[9,128]{1,0:T(8,128)S(1)} %broadcast_in_dim.2.turn, s32[8,256]{1,0:T(8,128)S(1)} %reshape.27.pairing, f32[9,6,1,2,8,256]{5,4,3,2,1,0:T(8,128)S(1)} %copy-done.1, f32[8,128]{1,0:T(8,128)S(1)} %get-tuple-element.13._), custom_call_target="tpu_custom_call" | custom-call | tf_op jit(solution)/shard_map/paired/pallas_call | solution.py:316
  9.2 2.2 %collective-permute-start.4 = (f32[9,6,8,128]{3,2,1,0:T(8,128)S(1)}, f32[9,6,8,128]{3,2,1,0:T(8,128)S(1)}, u32[]{:S(2)}, u32[]{:S(2)}) collective-permute-start(f32[9,6,8,128]{3,2,1,0:T(8,128)S(1)} %get-tuple-element.15), channel_id=1, source_target_pairs={{0,12},{1,13},{2,14},{3,15},{4,5},{5,4},{6,7},{7,6},{8,9},{9,8},{1... | collective-permute-start | bytes 663560 | tf_op jit(solution)/shard_map/ppermute | solution.py:390
  11.5 1.6 %collective-permute-start.3 = (f32[9,6,8,128]{3,2,1,0:T(8,128)S(1)}, f32[9,6,8,128]{3,2,1,0:T(8,128)S(1)}, u32[]{:S(2)}, u32[]{:S(2)}) collective-permute-start(f32[9,6,8,128]{3,2,1,0:T(8,128)S(1)} %get-tuple-element.14), channel_id=1, source_target_pairs={{0,12},{1,13},{2,14},{3,15},{4,5},{5,4},{6,7},{7,6},{8,9},{9,8},{1... | collective-permute-start | bytes 663560 | tf_op jit(solution)/shard_map/ppermute | solution.py:390
  13.1 0.0 collective-permute-start.1
  13.1 1.2 %collective-permute-done.1.span_ghost = f32[8,128]{1,0:T(8,128)S(1)} collective-permute-done((f32[8,128]{1,0:T(8,128)S(1)}, f32[8,128]{1,0:T(8,128)S(1)}, u32[]{:S(2)}, u32[]{:S(2)}) %collective-permute-start.1) | collective-permute-done | bytes 4128 | tf_op jit(solution)/shard_map/ppermute | solution.py:376
  14.3 1.5 %collective-permute-start = (f32[108,256]{1,0:T(8,128)S(1)}, f32[108,256]{1,0:T(8,128)S(1)}, u32[]{:S(2)}, u32[]{:S(2)}) collective-permute-start(f32[108,256]{1,0:T(8,128)S(1)} %get-tuple-element.12), channel_id=1, source_target_pairs={{0,2},{2,0},{4,6},{6,4},{8,10},{10,8},{12,14},{14,12},{1,3},{3,1},... | collective-permute-start | bytes 331784 | tf_op jit(solution)/shard_map/ppermute | solution.py:375
  15.8 3.7 %collective-permute-done.axial_ghost = f32[108,256]{1,0:T(8,128)S(1)} collective-permute-done((f32[108,256]{1,0:T(8,128)S(1)}, f32[108,256]{1,0:T(8,128)S(1)}, u32[]{:S(2)}, u32[]{:S(2)}) %collective-permute-start) | collective-permute-done | bytes 110624 | tf_op jit(solution)/shard_map/ppermute | solution.py:375
  19.5 0.0 copy-done.2
  19.5 0.0 copy-start.3
  19.5 1.2 %copy-done.3 = f32[9,6,1,2,8,256]{5,4,3,2,1,0:T(8,128)S(1)} copy-done((f32[9,6,1,2,8,256]{5,4,3,2,1,0:T(8,128)S(1)}, f32[9,6,1,2,8,256]{5,4,3,2,1,0:T(8,128)}, u32[]{:S(2)}) %copy-start.3) | copy-done | bytes 884760
  20.7 1.8 %base.1.partial = f32[9,6,2,8,256]{4,3,2,1,0:T(8,128)S(1)} custom-call(f32[9,6,1,2,8,256]{5,4,3,2,1,0:T(8,128)S(1)} %copy-done.1, f32[9,6,1,2,8,256]{5,4,3,2,1,0:T(8,128)S(1)} %copy-done.3, f32[6,6,1,2,8,256]{5,4,3,2,1,0:T(8,128)S(1)} %copy-done.2, f32[108,256]{1,0:T(8,128)S(1)} %collective-permute-done.axial_ghost, ...), custom_call_target="tpu_custom_call" | custom-call | tf_op jit(solution)/shard_map/base/pallas_call | solution.py:316
  22.4 0.0 collective-permute-done.5.ghost
  22.5 1.7 %near.1 = (f32[9,6,1,2,8,256]{5,4,3,2,1,0:T(8,128)}, f32[9,6,1,2,8,256]{5,4,3,2,1,0:T(8,128)}) custom-call(f32[9,6,2,8,256]{4,3,2,1,0:T(8,128)S(1)} %base.1.partial, f32[9,6,1,2,8,256]{5,4,3,2,1,0:T(8,128)S(1)} %copy-done.1, f32[6,6,1,2,8,256]{5,4,3,2,1,0:T(8,128)S(1)} %copy-done.2, f32[9,6,8,256]{3,2,1,0:T(8,128)S(1)} %collective-permute-done.5.ghost), custom_call_target="tpu_custom_call" | custom-call | tf_op jit(solution)/shard_map/near/pallas_call | solution.py:316
  24.2 0.0 collective-permute-done.4.paired
  24.2 0.0 collective-permute-done.2.middle
  24.2 1.2 %far.2 = (f32[9,6,1,2,8,256]{5,4,3,2,1,0:T(8,128)}, f32[9,6,1,2,8,256]{5,4,3,2,1,0:T(8,128)}) custom-call(f32[9,6,2,8,256]{4,3,2,1,0:T(8,128)S(1)} %base.1.partial, f32[9,6,1,2,8,256]{5,4,3,2,1,0:T(8,128)S(1)} %copy-done.1, f32[6,6,1,2,8,256]{5,4,3,2,1,0:T(8,128)S(1)} %copy-done.2, ...), custom_call_target="tpu_custom_call", output_to_operand_aliasing={{0}: (5, {}), {1}: (6, {})} | custom-call | tf_op jit(solution)/shard_map/far/pallas_call | solution.py:316
  25.4 1.5 %collective-permute-done.3.paired = f32[9,6,8,128]{3,2,1,0:T(8,128)S(1)} collective-permute-done((f32[9,6,8,128]{3,2,1,0:T(8,128)S(1)}, f32[9,6,8,128]{3,2,1,0:T(8,128)S(1)}, u32[]{:S(2)}, u32[]{:S(2)}) %collective-permute-start.3) | collective-permute-done | bytes 221216 | tf_op jit(solution)/shard_map/ppermute | solution.py:390
  26.9 1.2 %far.3 = (f32[9,6,1,2,8,256]{5,4,3,2,1,0:T(8,128)}, f32[9,6,1,2,8,256]{5,4,3,2,1,0:T(8,128)}) custom-call(f32[9,6,2,8,256]{4,3,2,1,0:T(8,128)S(1)} %base.1.partial, f32[9,6,1,2,8,256]{5,4,3,2,1,0:T(8,128)S(1)} %copy-done.1, f32[6,6,1,2,8,256]{5,4,3,2,1,0:T(8,128)S(1)} %copy-done.2, ...), custom_call_target="tpu_custom_call", output_to_operand_aliasing={{0}: (5, {}), {1}: (6, {})} | custom-call | tf_op jit(solution)/shard_map/far/pallas_call | solution.py:316
  (6 shorter events, 0.1 us)
Async XLA Ops:
  0.6 1.2 %copy-start = (f32[9,6,1,2,8,256]{5,4,3,2,1,0:T(8,128)S(1)}, f32[9,6,1,2,8,256]{5,4,3,2,1,0:T(8,128)}, u32[]{:S(2)}) copy-start(f32[9,6,1,2,8,256]{5,4,3,2,1,0:T(8,128)} %state.15) | copy-start | bytes 2654212
  1.8 20.6 %collective-permute-start.5 = (f32[9,6,8,256]{3,2,1,0:T(8,128)S(1)}, f32[9,6,8,256]{3,2,1,0:T(8,128)S(1)}, u32[]{:S(2)}, u32[]{:S(2)}) collective-permute-start(f32[9,6,8,256]{3,2,1,0:T(8,128)S(1)} %near_layer.1.refs_0_), channel_id=1, source_target_pairs={{0,4},{2,6},{4,0},{6,2},{8,12},{10,14},{12,8},{14,10},{1,5},{3,7},... | collective-permute-start | bytes 1327112 | tf_op jit(solution)/shard_map/ppermute | solution.py:361
  5.0 1.2 %copy-start.1 = (f32[9,6,1,2,8,256]{5,4,3,2,1,0:T(8,128)S(1)}, f32[9,6,1,2,8,256]{5,4,3,2,1,0:T(8,128)}, u32[]{:S(2)}) copy-start(f32[9,6,1,2,8,256]{5,4,3,2,1,0:T(8,128)} %state.15) | copy-start | bytes 2654212
  5.0 19.2 %collective-permute-start.2 = (f32[9,6,8,256]{3,2,1,0:T(8,128)S(1)}, f32[9,6,8,256]{3,2,1,0:T(8,128)S(1)}, u32[]{:S(2)}, u32[]{:S(2)}) collective-permute-start(f32[9,6,8,256]{3,2,1,0:T(8,128)S(1)} %far_layer.1._), channel_id=1, source_target_pairs={{0,1},{1,0},{2,3},{3,2},{4,8},{5,9},{6,10},{7,11},{8,4},{9,5},{10,... | collective-permute-start | bytes 1327112 | tf_op jit(solution)/shard_map/ppermute | solution.py:365
  5.1 0.7 %copy-start.5 = (s32[4]{0:T(128)S(1)}, s32[4]{0:T(128)}, u32[]{:S(2)}) copy-start(s32[4]{0:T(128)} %param.8) | copy-start | bytes 52
  5.1 0.8 %copy-start.4 = (s32[2048]{0:T(1024)S(1)}, s32[2048]{0:T(1024)}, u32[]{:S(2)}) copy-start(s32[2048]{0:T(1024)} %param.9) | copy-start | bytes 24580
  5.3 14.2 %copy-start.2 = (f32[6,6,1,2,8,256]{5,4,3,2,1,0:T(8,128)S(1)}, f32[6,6,1,2,8,256]{5,4,3,2,1,0:T(8,128)}, u32[]{:S(2)}) copy-start(f32[6,6,1,2,8,256]{5,4,3,2,1,0:T(8,128)} %matrix.7) | copy-start | bytes 1769476
  9.2 14.9 %collective-permute-start.4 = (f32[9,6,8,128]{3,2,1,0:T(8,128)S(1)}, f32[9,6,8,128]{3,2,1,0:T(8,128)S(1)}, u32[]{:S(2)}, u32[]{:S(2)}) collective-permute-start(f32[9,6,8,128]{3,2,1,0:T(8,128)S(1)} %get-tuple-element.15), channel_id=1, source_target_pairs={{0,12},{1,13},{2,14},{3,15},{4,5},{5,4},{6,7},{7,6},{8,9},{9,8},{1... | collective-permute-start | bytes 663560 | tf_op jit(solution)/shard_map/ppermute | solution.py:390
  11.5 15.4 %collective-permute-start.3 = (f32[9,6,8,128]{3,2,1,0:T(8,128)S(1)}, f32[9,6,8,128]{3,2,1,0:T(8,128)S(1)}, u32[]{:S(2)}, u32[]{:S(2)}) collective-permute-start(f32[9,6,8,128]{3,2,1,0:T(8,128)S(1)} %get-tuple-element.14), channel_id=1, source_target_pairs={{0,12},{1,13},{2,14},{3,15},{4,5},{5,4},{6,7},{7,6},{8,9},{9,8},{1... | collective-permute-start | bytes 663560 | tf_op jit(solution)/shard_map/ppermute | solution.py:390
  13.1 1.2 %collective-permute-start.1 = (f32[8,128]{1,0:T(8,128)S(1)}, f32[8,128]{1,0:T(8,128)S(1)}, u32[]{:S(2)}, u32[]{:S(2)}) collective-permute-start(f32[8,128]{1,0:T(8,128)S(1)} %get-tuple-element.13._), channel_id=1, source_target_pairs={{0,1},{1,0},{2,3},{3,2},{4,5},{5,4},{6,7},{7,6},{8,9},{9,8},{10,11... | collective-permute-start | bytes 12296 | tf_op jit(solution)/shard_map/ppermute | solution.py:376
  14.3 5.2 %collective-permute-start = (f32[108,256]{1,0:T(8,128)S(1)}, f32[108,256]{1,0:T(8,128)S(1)}, u32[]{:S(2)}, u32[]{:S(2)}) collective-permute-start(f32[108,256]{1,0:T(8,128)S(1)} %get-tuple-element.12), channel_id=1, source_target_pairs={{0,2},{2,0},{4,6},{6,4},{8,10},{10,8},{12,14},{14,12},{1,3},{3,1},... | collective-permute-start | bytes 331784 | tf_op jit(solution)/shard_map/ppermute | solution.py:375
  19.5 1.2 %copy-start.3 = (f32[9,6,1,2,8,256]{5,4,3,2,1,0:T(8,128)S(1)}, f32[9,6,1,2,8,256]{5,4,3,2,1,0:T(8,128)}, u32[]{:S(2)}) copy-start(f32[9,6,1,2,8,256]{5,4,3,2,1,0:T(8,128)} %source.1) | copy-start | bytes 2654212

commit v5 on v4

--- a/solution.py
+++ b/solution.py
@@ -258,9 +258,15 @@
     instances, variables = state.shape[:2]
     lanes = slice(t * LANES, (t + 1) * LANES)
     copies = [
-        pltpu.make_async_copy(buffers.at[n], whole.at[:, :, 0, c, :, lanes], sems.at[n])
-        for n, whole in enumerate((residual, updated))
+        pltpu.make_async_copy(buffers.at[0], residual.at[:, :, 0, c, :, lanes], sems.at[0])
     ]
+    cut = variables // 2
+    for n, part in enumerate((slice(0, cut), slice(cut, variables)), 1):
+        copies.append(
+            pltpu.make_async_copy(
+                buffers.at[1, :, part], updated.at[:, part, 0, c, :, lanes], sems.at[n]
+            )
+        )
     values = []
     for i in range(instances):
         values.append([])
@@ -270,10 +276,12 @@
             values[i].append(value)
     copies[0].start()
     update = solve_tile(values, lambda v, w: matrix[v, w, 0, c, :, lanes], (instances, variables))
-    for i in range(instances):
-        for v in range(variables):
+    for v in range(variables):
+        for i in range(instances):
             buffers[1, i, v] = state[i, v, 0, c, :, lanes] + update[i][v]
-    copies[1].start()
+        if v == cut - 1:
+            copies[1].start()
+    copies[2].start()
     return copies
 
 
@@ -405,7 +413,7 @@
         [out, out],
         "vvvv",
         "aa",
-        [pltpu.VMEM((tiles,) + tile, jnp.float32), pltpu.SemaphoreType.DMA((tiles, 2))],
+        [pltpu.VMEM((tiles,) + tile, jnp.float32), pltpu.SemaphoreType.DMA((tiles, 3))],
     )
     for t, ghost in enumerate(paired_ghosts):
         residual, updated = call(
@@ -415,7 +423,7 @@
             [out, out],
             "vvvvvaa",
             "aa",
-            [pltpu.VMEM(tile, jnp.float32), pltpu.SemaphoreType.DMA((2,))],
+            [pltpu.VMEM(tile, jnp.float32), pltpu.SemaphoreType.DMA((3,))],
             {5: 0, 6: 1},
         )
     return updated, residual

time: 28.3 us -> 28.2 us (level)
  no operation moved by 1% of the time
where the time goes in v5:
time: 28.2 us; the launch traced here: 28 us
  Pallas kernels  9.06 us (32%)
  starting transfers between devices  8.54 us (30%)
  waiting for transfers between devices  6.47 us (23%)
  local copies, waits for them, and re-layouts  3.02 us (11%)
  between operations  0.77 us (3%)
    pallas_call x8, Pallas kernels, call(): pl.pallas_call(kernel, name=name, in_specs=[kinds[k] for k in ins], out_s...  9.06 us
    ppermute x2, starting transfers between devices, shards(): lax.ppermute(face, both, far_route(True))  3.89 us
    ppermute x1, waiting for transfers between devices, shards(): axial_ghost = lax.ppermute(axial_face, 'blocks', axial_route)  3.73 us
    ppermute x1, starting transfers between devices, shards(): near_ghost = lax.ppermute(near_face, 'blocks', near_route)  3.09 us
    unnamed x12, local copies, waits for them, and re-layouts  2.94 us
    ppermute x2, waiting for transfers between devices, shards(): lax.ppermute(face, both, far_route(True))  1.57 us
    ppermute x1, starting transfers between devices, shards(): axial_ghost = lax.ppermute(axial_face, 'blocks', axial_route)  1.49 us
    ppermute x1, waiting for transfers between devices, shards(): span_ghost = lax.ppermute(span_face, 'span', [(0, 1), (1, 0)])  1.16 us
  transfers between devices with their start and end apart: 6, of which 3 were waited for; matrix products, arithmetic and copies ran while one was open for 1% of the time, Pallas kernels for 28%

profile of v5, /device:TPU:0, one launch (start us, length us, event | category | flops | bytes accessed | tf_op | source)
XLA Modules:
  0.0 28.0 jit_solution(8155723785246253322)
XLA Ops:
  0.6 0.0 copy-start
  0.6 1.2 %copy-done = f32[9,6,1,2,8,256]{5,4,3,2,1,0:T(8,128)S(1)} copy-done((f32[9,6,1,2,8,256]{5,4,3,2,1,0:T(8,128)S(1)}, f32[9,6,1,2,8,256]{5,4,3,2,1,0:T(8,128)}, u32[]{:S(2)}) %copy-start) | copy-done | bytes 884760
  1.8 3.1 %collective-permute-start.5 = (f32[9,6,8,256]{3,2,1,0:T(8,128)S(1)}, f32[9,6,8,256]{3,2,1,0:T(8,128)S(1)}, u32[]{:S(2)}, u32[]{:S(2)}) collective-permute-start(f32[9,6,8,256]{3,2,1,0:T(8,128)S(1)} %near_layer.1.refs_0_), channel_id=1, source_target_pairs={{0,4},{2,6},{4,0},{6,2},{8,12},{10,14},{12,8},{14,10},{1,5},{3,7},... | collective-permute-start | bytes 1327112 | tf_op jit(solution)/shard_map/ppermute | solution.py:369
  5.0 0.0 copy-start.1
  5.0 0.1 collective-permute-start.2
  5.1 0.0 copy-start.5
  5.1 0.0 copy-start.4
  5.1 0.2 faces.1
  5.3 0.0 copy-start.2
  5.3 0.4 %copy-done.5 = s32[4]{0:T(128)S(1)} copy-done((s32[4]{0:T(128)S(1)}, s32[4]{0:T(128)}, u32[]{:S(2)}) %copy-start.5) | copy-done | bytes 40
  5.8 0.0 copy-done.4
  5.8 0.1 fusion.1
  6.0 0.1 broadcast_in_dim.2.turn
  6.1 0.1 copy-done.1
  6.2 3.1 %paired.1 = (f32[9,6,8,128]{3,2,1,0:T(8,128)S(1)}, f32[9,6,8,128]{3,2,1,0:T(8,128)S(1)}) custom-call(f32[9,128]{1,0:T(8,128)S(1)} %broadcast_in_dim.2.turn, s32[8,256]{1,0:T(8,128)S(1)} %reshape.27.pairing, f32[9,6,1,2,8,256]{5,4,3,2,1,0:T(8,128)S(1)} %copy-done.1, f32[8,128]{1,0:T(8,128)S(1)} %get-tuple-element.13._), custom_call_target="tpu_custom_call" | custom-call | tf_op jit(solution)/shard_map/paired/pallas_call | solution.py:324
  9.2 2.2 %collective-permute-start.4 = (f32[9,6,8,128]{3,2,1,0:T(8,128)S(1)}, f32[9,6,8,128]{3,2,1,0:T(8,128)S(1)}, u32[]{:S(2)}, u32[]{:S(2)}) collective-permute-start(f32[9,6,8,128]{3,2,1,0:T(8,128)S(1)} %get-tuple-element.15), channel_id=1, source_target_pairs={{0,12},{1,13},{2,14},{3,15},{4,5},{5,4},{6,7},{7,6},{8,9},{9,8},{1... | collective-permute-start | bytes 663560 | tf_op jit(solution)/shard_map/ppermute | solution.py:398
  11.5 1.6 %collective-permute-start.3 = (f32[9,6,8,128]{3,2,1,0:T(8,128)S(1)}, f32[9,6,8,128]{3,2,1,0:T(8,128)S(1)}, u32[]{:S(2)}, u32[]{:S(2)}) collective-permute-start(f32[9,6,8,128]{3,2,1,0:T(8,128)S(1)} %get-tuple-element.14), channel_id=1, source_target_pairs={{0,12},{1,13},{2,14},{3,15},{4,5},{5,4},{6,7},{7,6},{8,9},{9,8},{1... | collective-permute-start | bytes 663560 | tf_op jit(solution)/shard_map/ppermute | solution.py:398
  13.1 0.0 collective-permute-start.1
  13.1 1.2 %collective-permute-done.1.span_ghost = f32[8,128]{1,0:T(8,128)S(1)} collective-permute-done((f32[8,128]{1,0:T(8,128)S(1)}, f32[8,128]{1,0:T(8,128)S(1)}, u32[]{:S(2)}, u32[]{:S(2)}) %collective-permute-start.1) | collective-permute-done | bytes 4128 | tf_op jit(solution)/shard_map/ppermute | solution.py:384
  14.3 1.5 %collective-permute-start = (f32[108,256]{1,0:T(8,128)S(1)}, f32[108,256]{1,0:T(8,128)S(1)}, u32[]{:S(2)}, u32[]{:S(2)}) collective-permute-start(f32[108,256]{1,0:T(8,128)S(1)} %get-tuple-element.12), channel_id=1, source_target_pairs={{0,2},{2,0},{4,6},{6,4},{8,10},{10,8},{12,14},{14,12},{1,3},{3,1},... | collective-permute-start | bytes 331784 | tf_op jit(solution)/shard_map/ppermute | solution.py:383
  15.8 3.7 %collective-permute-done.axial_ghost = f32[108,256]{1,0:T(8,128)S(1)} collective-permute-done((f32[108,256]{1,0:T(8,128)S(1)}, f32[108,256]{1,0:T(8,128)S(1)}, u32[]{:S(2)}, u32[]{:S(2)}) %collective-permute-start) | collective-permute-done | bytes 110624 | tf_op jit(solution)/shard_map/ppermute | solution.py:383
  19.5 0.0 copy-done.2
  19.5 0.0 copy-start.3
  19.5 1.2 %copy-done.3 = f32[9,6,1,2,8,256]{5,4,3,2,1,0:T(8,128)S(1)} copy-done((f32[9,6,1,2,8,256]{5,4,3,2,1,0:T(8,128)S(1)}, f32[9,6,1,2,8,256]{5,4,3,2,1,0:T(8,128)}, u32[]{:S(2)}) %copy-start.3) | copy-done | bytes 884760
  20.7 1.8 %base.1.partial = f32[9,6,2,8,256]{4,3,2,1,0:T(8,128)S(1)} custom-call(f32[9,6,1,2,8,256]{5,4,3,2,1,0:T(8,128)S(1)} %copy-done.1, f32[9,6,1,2,8,256]{5,4,3,2,1,0:T(8,128)S(1)} %copy-done.3, f32[6,6,1,2,8,256]{5,4,3,2,1,0:T(8,128)S(1)} %copy-done.2, f32[108,256]{1,0:T(8,128)S(1)} %collective-permute-done.axial_ghost, ...), custom_call_target="tpu_custom_call" | custom-call | tf_op jit(solution)/shard_map/base/pallas_call | solution.py:324
  22.4 0.0 collective-permute-done.5.ghost
  22.5 1.7 %near.1 = (f32[9,6,1,2,8,256]{5,4,3,2,1,0:T(8,128)}, f32[9,6,1,2,8,256]{5,4,3,2,1,0:T(8,128)}) custom-call(f32[9,6,2,8,256]{4,3,2,1,0:T(8,128)S(1)} %base.1.partial, f32[9,6,1,2,8,256]{5,4,3,2,1,0:T(8,128)S(1)} %copy-done.1, f32[6,6,1,2,8,256]{5,4,3,2,1,0:T(8,128)S(1)} %copy-done.2, f32[9,6,8,256]{3,2,1,0:T(8,128)S(1)} %collective-permute-done.5.ghost), custom_call_target="tpu_custom_call" | custom-call | tf_op jit(solution)/shard_map/near/pallas_call | solution.py:324
  24.1 0.0 collective-permute-done.4.paired
  24.1 0.0 collective-permute-done.2.middle
  24.1 1.1 %far.2 = (f32[9,6,1,2,8,256]{5,4,3,2,1,0:T(8,128)}, f32[9,6,1,2,8,256]{5,4,3,2,1,0:T(8,128)}) custom-call(f32[9,6,2,8,256]{4,3,2,1,0:T(8,128)S(1)} %base.1.partial, f32[9,6,1,2,8,256]{5,4,3,2,1,0:T(8,128)S(1)} %copy-done.1, f32[6,6,1,2,8,256]{5,4,3,2,1,0:T(8,128)S(1)} %copy-done.2, ...), custom_call_target="tpu_custom_call", output_to_operand_aliasing={{0}: (5, {}), {1}: (6, {})} | custom-call | tf_op jit(solution)/shard_map/far/pallas_call | solution.py:324
  25.3 1.6 %collective-permute-done.3.paired = f32[9,6,8,128]{3,2,1,0:T(8,128)S(1)} collective-permute-done((f32[9,6,8,128]{3,2,1,0:T(8,128)S(1)}, f32[9,6,8,128]{3,2,1,0:T(8,128)S(1)}, u32[]{:S(2)}, u32[]{:S(2)}) %collective-permute-start.3) | collective-permute-done | bytes 221216 | tf_op jit(solution)/shard_map/ppermute | solution.py:398
  26.9 1.1 %far.3 = (f32[9,6,1,2,8,256]{5,4,3,2,1,0:T(8,128)}, f32[9,6,1,2,8,256]{5,4,3,2,1,0:T(8,128)}) custom-call(f32[9,6,2,8,256]{4,3,2,1,0:T(8,128)S(1)} %base.1.partial, f32[9,6,1,2,8,256]{5,4,3,2,1,0:T(8,128)S(1)} %copy-done.1, f32[6,6,1,2,8,256]{5,4,3,2,1,0:T(8,128)S(1)} %copy-done.2, ...), custom_call_target="tpu_custom_call", output_to_operand_aliasing={{0}: (5, {}), {1}: (6, {})} | custom-call | tf_op jit(solution)/shard_map/far/pallas_call | solution.py:324
  (6 shorter events, 0.1 us)
Async XLA Ops:
  0.6 1.2 %copy-start = (f32[9,6,1,2,8,256]{5,4,3,2,1,0:T(8,128)S(1)}, f32[9,6,1,2,8,256]{5,4,3,2,1,0:T(8,128)}, u32[]{:S(2)}) copy-start(f32[9,6,1,2,8,256]{5,4,3,2,1,0:T(8,128)} %state.15) | copy-start | bytes 2654212
  1.8 20.6 %collective-permute-start.5 = (f32[9,6,8,256]{3,2,1,0:T(8,128)S(1)}, f32[9,6,8,256]{3,2,1,0:T(8,128)S(1)}, u32[]{:S(2)}, u32[]{:S(2)}) collective-permute-start(f32[9,6,8,256]{3,2,1,0:T(8,128)S(1)} %near_layer.1.refs_0_), channel_id=1, source_target_pairs={{0,4},{2,6},{4,0},{6,2},{8,12},{10,14},{12,8},{14,10},{1,5},{3,7},... | collective-permute-start | bytes 1327112 | tf_op jit(solution)/shard_map/ppermute | solution.py:369
  5.0 1.2 %copy-start.1 = (f32[9,6,1,2,8,256]{5,4,3,2,1,0:T(8,128)S(1)}, f32[9,6,1,2,8,256]{5,4,3,2,1,0:T(8,128)}, u32[]{:S(2)}) copy-start(f32[9,6,1,2,8,256]{5,4,3,2,1,0:T(8,128)} %state.15) | copy-start | bytes 2654212
  5.0 19.2 %collective-permute-start.2 = (f32[9,6,8,256]{3,2,1,0:T(8,128)S(1)}, f32[9,6,8,256]{3,2,1,0:T(8,128)S(1)}, u32[]{:S(2)}, u32[]{:S(2)}) collective-permute-start(f32[9,6,8,256]{3,2,1,0:T(8,128)S(1)} %far_layer.1._), channel_id=1, source_target_pairs={{0,1},{1,0},{2,3},{3,2},{4,8},{5,9},{6,10},{7,11},{8,4},{9,5},{10,... | collective-permute-start | bytes 1327112 | tf_op jit(solution)/shard_map/ppermute | solution.py:373
  5.1 0.7 %copy-start.5 = (s32[4]{0:T(128)S(1)}, s32[4]{0:T(128)}, u32[]{:S(2)}) copy-start(s32[4]{0:T(128)} %param.8) | copy-start | bytes 52
  5.1 0.8 %copy-start.4 = (s32[2048]{0:T(1024)S(1)}, s32[2048]{0:T(1024)}, u32[]{:S(2)}) copy-start(s32[2048]{0:T(1024)} %param.9) | copy-start | bytes 24580
  5.3 14.2 %copy-start.2 = (f32[6,6,1,2,8,256]{5,4,3,2,1,0:T(8,128)S(1)}, f32[6,6,1,2,8,256]{5,4,3,2,1,0:T(8,128)}, u32[]{:S(2)}) copy-start(f32[6,6,1,2,8,256]{5,4,3,2,1,0:T(8,128)} %matrix.7) | copy-start | bytes 1769476
  9.2 14.9 %collective-permute-start.4 = (f32[9,6,8,128]{3,2,1,0:T(8,128)S(1)}, f32[9,6,8,128]{3,2,1,0:T(8,128)S(1)}, u32[]{:S(2)}, u32[]{:S(2)}) collective-permute-start(f32[9,6,8,128]{3,2,1,0:T(8,128)S(1)} %get-tuple-element.15), channel_id=1, source_target_pairs={{0,12},{1,13},{2,14},{3,15},{4,5},{5,4},{6,7},{7,6},{8,9},{9,8},{1... | collective-permute-start | bytes 663560 | tf_op jit(solution)/shard_map/ppermute | solution.py:398
  11.5 15.4 %collective-permute-start.3 = (f32[9,6,8,128]{3,2,1,0:T(8,128)S(1)}, f32[9,6,8,128]{3,2,1,0:T(8,128)S(1)}, u32[]{:S(2)}, u32[]{:S(2)}) collective-permute-start(f32[9,6,8,128]{3,2,1,0:T(8,128)S(1)} %get-tuple-element.14), channel_id=1, source_target_pairs={{0,12},{1,13},{2,14},{3,15},{4,5},{5,4},{6,7},{7,6},{8,9},{9,8},{1... | collective-permute-start | bytes 663560 | tf_op jit(solution)/shard_map/ppermute | solution.py:398
  13.1 1.2 %collective-permute-start.1 = (f32[8,128]{1,0:T(8,128)S(1)}, f32[8,128]{1,0:T(8,128)S(1)}, u32[]{:S(2)}, u32[]{:S(2)}) collective-permute-start(f32[8,128]{1,0:T(8,128)S(1)} %get-tuple-element.13._), channel_id=1, source_target_pairs={{0,1},{1,0},{2,3},{3,2},{4,5},{5,4},{6,7},{7,6},{8,9},{9,8},{10,11... | collective-permute-start | bytes 12296 | tf_op jit(solution)/shard_map/ppermute | solution.py:384
  14.3 5.2 %collective-permute-start = (f32[108,256]{1,0:T(8,128)S(1)}, f32[108,256]{1,0:T(8,128)S(1)}, u32[]{:S(2)}, u32[]{:S(2)}) collective-permute-start(f32[108,256]{1,0:T(8,128)S(1)} %get-tuple-element.12), channel_id=1, source_target_pairs={{0,2},{2,0},{4,6},{6,4},{8,10},{10,8},{12,14},{14,12},{1,3},{3,1},... | collective-permute-start | bytes 331784 | tf_op jit(solution)/shard_map/ppermute | solution.py:383
  19.5 1.2 %copy-start.3 = (f32[9,6,1,2,8,256]{5,4,3,2,1,0:T(8,128)S(1)}, f32[9,6,1,2,8,256]{5,4,3,2,1,0:T(8,128)}, u32[]{:S(2)}) copy-start(f32[9,6,1,2,8,256]{5,4,3,2,1,0:T(8,128)} %source.1) | copy-start | bytes 2654212
